TPU v7x, 32 devices: a whole 2x2x4 slice. The times are simulated.
32 devices in a mesh: dp: 8 (over z, y), expert: 4 (over x, core).
Axes of the slice: x: 2, y: 2, z: 4, core: 2. Of those that a mesh axis runs over, the one named last changes fastest.
Arguments:
- tokens: bfloat16 [4096, 2048], P(('dp', 'expert')), may hold values from -6 to 6
- expert_ids: int32 [4096, 2], P(('dp', 'expert')), may hold values from 0 to 3, all different within a row; in each aligned block of 128 rows (0 to 127, 128 to 255, ...) at most 66 rows name the same one
- gate_probs: bfloat16 [4096, 2], P(('dp', 'expert')), may hold values from 0.099609375 to 1
- w_gate: bfloat16 [4, 2048, 768], P('expert'), may hold values from -0.125 to 0.125
- w_up: bfloat16 [4, 2048, 768], P('expert'), may hold values from -0.125 to 0.125
- w_down: bfloat16 [4, 768, 2048], P('expert'), may hold values from -0.21875 to 0.21875
- teacher_queries: bfloat16 [4, 8, 2048], P('expert', 'dp'), may hold values from -6 to 6
- teacher_passages: bfloat16 [4, 16, 2048], P('expert', 'dp'), may hold values from -6 to 6
- positives: int32 [4, 8], P('expert', 'dp'), may hold values from 0 to 15
Outputs:
- moe_out: bfloat16 [4096, 2048], P(('dp', 'expert'))
- token_grad: bfloat16 [4096, 2048], P(('dp', 'expert'))
- gate_grad: float32 [4096, 2], P(('dp', 'expert'))
- query_loss: float32 [4, 8], P('expert', 'dp')
Inputs may be any that keep to these rules, and one draw needn't show every extreme that they name: `expert_ids`: each token names 2 different experts of its group; among the 128 tokens of one device no expert is named more than 66 times, a bound that some block reaches.
All inputs are finite; a program needn't handle non-finite values.
Results may differ from a plain program's by a relative error of at most 0.015.
Values may be sent and summed in bfloat16 or wider, within the bound.
A program may use at most 64 MiB of HBM per device.

v0:
```python
import jax
import jax.numpy as jnp
from jax import lax
from jax.sharding import PartitionSpec as P

QLEN = 32
PLEN = 48


student_scale = 50.0
teacher_scale = 80.0
loss_scale = 64.0
norm_eps = 1e-06


def silu_slope(pre_gate):
    sigmoid = jax.nn.sigmoid(pre_gate)
    return sigmoid * (1.0 + pre_gate * (1.0 - sigmoid))


def contract_lead(left_mat, right_mat):
    return lax.dot_general(
        left_mat, right_mat, (((0,), (0,)), ((), ())), preferred_element_type=jnp.float32
    )


def contract_last(left_mat, right_mat):
    return lax.dot_general(
        left_mat, right_mat, (((1,), (1,)), ((), ())), preferred_element_type=jnp.float32
    )


def unit_rows(values):
    as_float = values.astype(jnp.float32)
    inverse = lax.rsqrt(jnp.sum(as_float * as_float, axis=-1, keepdims=True) + norm_eps)
    return (as_float * inverse, inverse)


def unit_back(normed, inverse, grad_normed):
    return inverse * (grad_normed - normed * jnp.sum(normed * grad_normed, axis=-1, keepdims=True))


def shards(
    tokens,
    expert_ids,
    gate_probs,
    w_gate,
    w_up,
    w_down,
    teacher_queries,
    teacher_passages,
    positives,
):
    group_size = lax.axis_size("expert")
    tok_rows, model_width = tokens.shape
    top_count = expert_ids.shape[1]
    query_count = teacher_queries.shape[1]
    local_count = teacher_passages.shape[1]
    capacity = min(tok_rows, (tok_rows * top_count * 33 + 32 * group_size - 1) // (32 * group_size))
    slot_total = group_size * capacity
    flat_ids = expert_ids.reshape(-1)
    row_count = flat_ids.shape[0]
    expert_hits = (flat_ids[:, None] == jnp.arange(group_size, dtype=jnp.int32)[None, :]).astype(
        jnp.int32
    )
    earlier = jnp.cumsum(expert_hits, axis=0) - expert_hits
    slot_index = flat_ids * capacity + jnp.sum(earlier * expert_hits, axis=1)
    slot_source = (
        jnp.full((slot_total,), row_count, jnp.int32)
        .at[slot_index]
        .set(jnp.arange(row_count, dtype=jnp.int32))
    )
    padded_tokens = jnp.concatenate([tokens, jnp.zeros((1, model_width), tokens.dtype)], axis=0)
    send_rows = padded_tokens[slot_source // top_count].reshape(group_size, capacity, model_width)
    gate_flat = gate_probs.reshape(-1, 1).astype(jnp.float32)
    gate_mat = w_gate[0]
    up_mat = w_up[0]
    down_mat = w_down[0]
    arrived = lax.all_to_all(send_rows, "expert", split_axis=0, concat_axis=0, tiled=True)
    sources = arrived.shape[0]
    slot_count = arrived.shape[1]
    arrived_rows = arrived.reshape(-1, model_width)
    pre_gate = jnp.dot(arrived_rows, gate_mat, preferred_element_type=jnp.float32)
    pre_up = jnp.dot(arrived_rows, up_mat, preferred_element_type=jnp.float32)
    hidden = (jax.nn.silu(pre_gate) * pre_up).astype(jnp.bfloat16)
    expert_out = jnp.dot(hidden, down_mat, preferred_element_type=jnp.float32).astype(jnp.bfloat16)
    returned = lax.all_to_all(
        expert_out.reshape(sources, slot_count, model_width),
        "expert",
        split_axis=0,
        concat_axis=0,
        tiled=True,
    )
    saved_gate = pre_gate.reshape(sources, slot_count, -1)
    saved_up = pre_up.reshape(sources, slot_count, -1)
    token_out = returned.reshape(slot_total, model_width)[slot_index].astype(jnp.float32)
    moe_out = jnp.sum(
        (gate_flat * token_out).reshape(tok_rows, top_count, model_width), axis=1
    ).astype(jnp.bfloat16)
    moe_wide = moe_out.astype(jnp.float32)
    query_span = query_count * QLEN
    pooled_q = jnp.mean(moe_wide[:query_span].reshape(query_count, QLEN, model_width), axis=1)
    pooled_p = jnp.mean(moe_wide[query_span:].reshape(local_count, PLEN, model_width), axis=1)
    query_unit, query_inv = unit_rows(pooled_q)
    passage_unit, passage_inv = unit_rows(pooled_p)
    query_half = query_unit.astype(jnp.bfloat16)
    passage_half = passage_unit.astype(jnp.bfloat16)
    teacher_q_half = unit_rows(teacher_queries[0])[0].astype(jnp.bfloat16)
    teacher_p_half = unit_rows(teacher_passages[0])[0].astype(jnp.bfloat16)
    dp_count = lax.axis_size("dp")
    total_count = local_count * dp_count
    student_part = student_scale * contract_last(
        query_half, lax.all_gather(passage_half, "dp", axis=0, tiled=True)
    )
    teacher_part = teacher_scale * contract_last(
        teacher_q_half, lax.all_gather(teacher_p_half, "dp", axis=0, tiled=True)
    )
    student_exp = jnp.exp(student_part)
    teacher_exp = jnp.exp(teacher_part)
    student_total = jnp.sum(student_exp, axis=1)
    teacher_total = jnp.sum(teacher_exp, axis=1)
    cross_term = jnp.sum(teacher_exp * (teacher_part - student_part), axis=1)
    is_positive = positives[0][:, None] == jnp.arange(total_count, dtype=jnp.int32)[None, :]
    positive_score = jnp.sum(jnp.where(is_positive, student_part, 0.0), axis=1)
    query_loss = (
        2.0 * jnp.log(student_total)
        - positive_score
        + cross_term / teacher_total
        - jnp.log(teacher_total)
    )
    coeffs = (
        2.0 * student_exp / student_total[:, None]
        - teacher_exp / teacher_total[:, None]
        - is_positive.astype(jnp.float32)
    ).astype(jnp.bfloat16)
    columns = coeffs
    unit_q_grad = student_scale * jnp.dot(
        columns,
        lax.all_gather(passage_half, "dp", axis=0, tiled=True),
        preferred_element_type=jnp.float32,
    )
    columns = coeffs
    unit_p_grad = lax.psum_scatter(
        student_scale * contract_lead(columns, query_half), "dp", scatter_dimension=0, tiled=True
    )
    query_grad = unit_back(query_unit, query_inv, unit_q_grad)
    passage_grad = unit_back(passage_unit, passage_inv, unit_p_grad)
    out_grad = jnp.concatenate(
        [
            jnp.repeat(query_grad * (loss_scale / QLEN), QLEN, axis=0),
            jnp.repeat(passage_grad * (loss_scale / PLEN), PLEN, axis=0),
        ],
        axis=0,
    )
    grad_rep = jnp.repeat(out_grad, top_count, axis=0)
    routed_grad = (gate_flat * grad_rep).astype(jnp.bfloat16)
    padded_grad = jnp.concatenate([routed_grad, jnp.zeros((1, model_width), jnp.bfloat16)], axis=0)
    send_grads = padded_grad[slot_source].reshape(group_size, capacity, model_width)
    arrived_grad = lax.all_to_all(send_grads, "expert", split_axis=0, concat_axis=0, tiled=True)
    grad_rows = arrived_grad.reshape(-1, model_width)
    pre_gate = saved_gate.reshape(grad_rows.shape[0], -1)
    pre_up = saved_up.reshape(grad_rows.shape[0], -1)
    hidden_grad = contract_last(grad_rows, down_mat)
    gate_part = (hidden_grad * pre_up * silu_slope(pre_gate)).astype(jnp.bfloat16)
    up_part = (hidden_grad * jax.nn.silu(pre_gate)).astype(jnp.bfloat16)
    row_grad = (contract_last(gate_part, gate_mat) + contract_last(up_part, up_mat)).astype(
        jnp.bfloat16
    )
    back_grad = lax.all_to_all(
        row_grad.reshape(group_size, capacity, model_width),
        "expert",
        split_axis=0,
        concat_axis=0,
        tiled=True,
    )
    token_row_grad = back_grad.reshape(slot_total, model_width)[slot_index].astype(jnp.float32)
    token_grad = jnp.sum(token_row_grad.reshape(tok_rows, top_count, model_width), axis=1).astype(
        jnp.bfloat16
    )
    gate_grad = jnp.sum(token_out * grad_rep, axis=1).reshape(tok_rows, top_count)
    return (moe_out, token_grad, gate_grad, query_loss[None])


def solution(mesh):
    in_specs = (
        P(("dp", "expert"), None),
        P(("dp", "expert"), None),
        P(("dp", "expert"), None),
        P("expert", None, None),
        P("expert", None, None),
        P("expert", None, None),
        P("expert", "dp", None),
        P("expert", "dp", None),
        P("expert", "dp"),
    )
    out_specs = (
        P(("dp", "expert"), None),
        P(("dp", "expert"), None),
        P(("dp", "expert"), None),
        P("expert", "dp"),
    )
    return jax.shard_map(shards, mesh=mesh, in_specs=in_specs, out_specs=out_specs, check_vma=False)
```

profile of v0, /device:TPU:0, one launch (start us, length us, event | category | flops | bytes accessed | tf_op | source)
XLA Modules:
  0.0 316.5 jit_solution(11010284402743413873)
XLA Ops:
  14.5 6.0 %gather_fusion = bf16[264,2048]{1,0:T(8,128)(2,1)} fusion(bf16[129,2048]{1,0:T(8,128)(2,1)} %concatenate.9, s32[1024]{0:T(1024)S(1)} %get-tuple-element.28), kind=kCustom, calls=%fused_computation | custom fusion | bytes 2163744 | tf_op jit(solution)/shard_map/gather | solution.py:74
  20.5 2.6 reshape.259
  23.1 4.3 %all-to-all-start = ((bf16[4,66,2048]{2,1,0:T(8,128)(2,1)}), bf16[4,66,2048]{2,1,0:T(8,128)(2,1)}, u32[]{:S(2)}, u32[]{:S(2)}) async-start(bf16[4,66,2048]{2,1,0:T(8,128)(2,1)} %reshape.259), calls=%async_computation | async-start | bytes 2359296 | tf_op jit(solution)/shard_map/all_to_all | solution.py:79
  29.5 14.4 %all-to-all-done = bf16[4,66,2048]{2,1,0:T(8,128)(2,1)} async-done(((bf16[4,66,2048]{2,1,0:T(8,128)(2,1)}), bf16[4,66,2048]{2,1,0:T(8,128)(2,1)}, u32[]{:S(2)}, u32[]{:S(2)}) %all-to-all-start) | async-done | bytes 1081376 | tf_op jit(solution)/shard_map/all_to_all | solution.py:79
  43.9 2.6 reshape.260
  46.5 3.4 %fusion.10 = f32[264,768]{1,0:T(8,128)S(1)} fusion(bf16[264,2048]{1,0:T(8,128)(2,1)} %reshape.260, bf16[1,2048,768]{2,1,0:T(8,128)(2,1)} %param.12), kind=kOutput, calls=%fused_computation.15 | convolution fusion | flops 830472192 | bytes 5038080 | tf_op jit(solution)/shard_map/dot_general | solution.py:83
  54.0 2.6 reshape.261
  56.6 4.3 %all-to-all-start.1 = ((bf16[4,66,2048]{2,1,0:T(8,128)(2,1)}), bf16[4,66,2048]{2,1,0:T(8,128)(2,1)}, u32[]{:S(2)}, u32[]{:S(2)}) async-start(bf16[4,66,2048]{2,1,0:T(8,128)(2,1)} %reshape.261), calls=%async_computation.1 | async-start | bytes 2359296 | tf_op jit(solution)/shard_map/all_to_all | solution.py:87
  61.0 31.9 %all-gather.1 = bf16[8,2,2048]{2,1,0:T(2,128)(2,1)S(1)} all-gather(bf16[1,2,2048]{2,1,0:T(2,128)(2,1)S(1)} %fusion.33), channel_id=1, replica_groups=mesh['dp'=8,'expert'=4] {'dp'}, dimensions={0}, use_global_device_ids=true | all-gather | bytes 73728 | tf_op jit(solution)/shard_map/all_gather | solution.py:116
  94.4 2.6 reshape.262
  97.0 4.7 %gather_fusion.1 = bf16[256,2048]{1,0:T(8,128)(2,1)} fusion(bf16[264,2048]{1,0:T(8,128)(2,1)} %reshape.262, s32[1024]{0:T(1024)S(1)} %pad_clamp_fusion.1), kind=kCustom, calls=%fused_computation.1 | custom fusion | bytes 2098176 | tf_op jit(solution)/shard_map/gather | solution.py:96
  101.7 3.4 %reshape.271 = f32[128,2,2048]{2,1,0:T(2,128)} reshape(bf16[256,2048]{1,0:T(8,128)(2,1)} %gather_fusion.1) | data formatting | bytes 3145728 | tf_op jit(solution)/shard_map/convert_element_type | solution.py:96
  105.1 4.8 %multiply_reduce_fusion.1 = bf16[128,2048]{1,0:T(8,128)(2,1)S(1)} fusion(f32[128,2,2048]{2,1,0:T(2,128)} %reshape.271, f32[128,2]{1,0:T(8,128)S(1)} %copy.24), kind=kLoop, calls=%fused_computation.22 | loop fusion | flops 786432 | bytes 2622464 | tf_op jit(solution)/shard_map/reduce_sum | solution.py:97
  113.6 30.7 %all-gather = bf16[8,2,2048]{2,1,0:T(2,128)(2,1)S(1)} all-gather(bf16[1,2,2048]{2,1,0:T(2,128)(2,1)S(1)} %fusion.34), channel_id=1, replica_groups=mesh['dp'=8,'expert'=4] {'dp'}, dimensions={0}, use_global_device_ids=true | all-gather | bytes 73728 | tf_op jit(solution)/shard_map/all_gather | solution.py:113
  151.0 70.5 %all-reduce.5.cloned.1.call-done = f32[16,2048]{1,0:T(8,128)} async-done(((f32[16,2048]{1,0:T(8,128)}), f32[16,2048]{1,0:T(8,128)}) %all-reduce.5.cloned.1.call-update) | async-done | bytes 131088
  226.1 3.7 %reshape.266 = f32[256,2048]{1,0:T(8,128)} reshape(f32[128,2,2048]{2,1,0:T(2,128)} %broadcast_in_dim.19) | data formatting | bytes 4194304 | tf_op jit(solution)/shard_map/reshape | solution.py:155
  233.0 6.2 %gather_fusion.2 = bf16[264,2048]{1,0:T(8,128)(2,1)} fusion(bf16[257,2048]{1,0:T(8,128)(2,1)} %concatenate.11, s32[1024]{0:T(1024)S(1)} %get-tuple-element.27), kind=kCustom, calls=%fused_computation.2 | custom fusion | bytes 2163744 | tf_op jit(solution)/shard_map/gather | solution.py:158
  241.8 20.2 %all_to_all.20 = bf16[4,66,2048]{2,1,0:T(8,128)(2,1)} all-to-all(bf16[4,66,2048]{2,1,0:T(8,128)(2,1)} %reshape.267), channel_id=1, replica_groups=mesh['dp'=8,'expert'=4] {'expert'}, dimensions={0} | all-to-all | bytes 2162688 | tf_op jit(solution)/shard_map/all_to_all | solution.py:159
  271.3 2.6 reshape.269
  273.9 4.5 %all-to-all-start.3 = ((bf16[4,66,2048]{2,1,0:T(8,128)(2,1)}), bf16[4,66,2048]{2,1,0:T(8,128)(2,1)}, u32[]{:S(2)}, u32[]{:S(2)}) async-start(bf16[4,66,2048]{2,1,0:T(8,128)(2,1)} %reshape.269), calls=%async_computation.3 | async-start | bytes 2359296 | tf_op jit(solution)/shard_map/all_to_all | solution.py:169
  282.5 11.6 %all-to-all-done.3 = bf16[4,66,2048]{2,1,0:T(8,128)(2,1)} async-done(((bf16[4,66,2048]{2,1,0:T(8,128)(2,1)}), bf16[4,66,2048]{2,1,0:T(8,128)(2,1)}, u32[]{:S(2)}, u32[]{:S(2)}) %all-to-all-start.3) | async-done | bytes 1081376 | tf_op jit(solution)/shard_map/all_to_all | solution.py:169
  294.1 2.6 reshape.270
  296.7 4.7 %gather_fusion.3 = bf16[256,2048]{1,0:T(8,128)(2,1)} fusion(bf16[264,2048]{1,0:T(8,128)(2,1)} %reshape.270, s32[1024]{0:T(1024)S(1)} %pad_clamp_fusion.1), kind=kCustom, calls=%fused_computation.3 | custom fusion | bytes 2098176 | tf_op jit(solution)/shard_map/gather | solution.py:176
  303.9 4.6 %reduce_sum.164 = bf16[128,2048]{1,0:T(8,128)(2,1)} reduce(bf16[128,2,2048]{2,1,0:T(2,128)(2,1)} %gather.18, bf16[]{:T(256)} %constant.19.clone.1), dimensions={1}, to_apply=%region_16.17 | reduce | flops 262144 | bytes 1572866 | tf_op jit(solution)/shard_map/reduce_sum | solution.py:177
  (97 shorter events, 45.6 us)
Async XLA Ops:
  7.2 44.7 %copy-start = (bf16[1,768,2048]{2,1,0:T(8,128)(2,1)S(1)}, bf16[1,768,2048]{2,1,0:T(8,128)(2,1)}, u32[]{:S(2)}) copy-start(bf16[1,768,2048]{2,1,0:T(8,128)(2,1)} %param.14) | copy-start | bytes 9437188
  20.5 7.5 %copy-start.4 = (bf16[1,1,2048]{2,1,0:T(2,128)(2,1)S(1)}, bf16[1,1,2048]{2,1,0:T(2,128)(2,1)}, u32[]{:S(2)}) copy-start(bf16[1,1,2048]{2,1,0:T(2,128)(2,1)} %param.15) | copy-start | bytes 12292
  20.5 8.9 %copy-start.3 = (bf16[1,2,2048]{2,1,0:T(2,128)(2,1)S(1)}, bf16[1,2,2048]{2,1,0:T(2,128)(2,1)}, u32[]{:S(2)}) copy-start(bf16[1,2,2048]{2,1,0:T(2,128)(2,1)} %param.16) | copy-start | bytes 24580
  23.1 20.8 %all-to-all-start = ((bf16[4,66,2048]{2,1,0:T(8,128)(2,1)}), bf16[4,66,2048]{2,1,0:T(8,128)(2,1)}, u32[]{:S(2)}, u32[]{:S(2)}) async-start(bf16[4,66,2048]{2,1,0:T(8,128)(2,1)} %reshape.259), calls=%async_computation | async-start | bytes 2359296 | tf_op jit(solution)/shard_map/all_to_all | solution.py:79
  46.5 3.4 %copy-start.2 = (bf16[264,2048]{1,0:T(8,128)(2,1)S(1)}, bf16[264,2048]{1,0:T(8,128)(2,1)}, u32[]{:S(2)}) copy-start(bf16[264,2048]{1,0:T(8,128)(2,1)} %reshape.260) | copy-start | bytes 3244036
  46.5 3.5 %copy-start.6 = (bf16[1,2048,768]{2,1,0:T(8,128)(2,1)S(1)}, bf16[1,2048,768]{2,1,0:T(8,128)(2,1)}, u32[]{:S(2)}) copy-start(bf16[1,2048,768]{2,1,0:T(8,128)(2,1)} %param.13) | copy-start | bytes 9437188
  50.0 1.0 copy-start.10
  51.0 0.9 copy-start.12
  54.0 38.9 %copy-start.5 = (bf16[128,2]{0,1:T(2,128)(2,1)S(1)}, bf16[128,2]{0,1:T(2,128)(2,1)}, u32[]{:S(2)}) copy-start(bf16[128,2]{0,1:T(2,128)(2,1)} %param.11) | copy-start | bytes 1540
  54.0 39.2 %copy-start.9 = (u32[32]{0:T(128)S(1)}, u32[32]{0:T(128)}, u32[]{:S(2)}) copy-start(u32[32]{0:T(128)} %constant.77) | copy-start | bytes 388
  56.6 37.8 %all-to-all-start.1 = ((bf16[4,66,2048]{2,1,0:T(8,128)(2,1)}), bf16[4,66,2048]{2,1,0:T(8,128)(2,1)}, u32[]{:S(2)}, u32[]{:S(2)}) async-start(bf16[4,66,2048]{2,1,0:T(8,128)(2,1)} %reshape.261), calls=%async_computation.1 | async-start | bytes 2359296 | tf_op jit(solution)/shard_map/all_to_all | solution.py:87
  60.9 160.6 %all-reduce.5.cloned.1.call-start = ((), (), s32[]{:S(2)}) async-start(), calls=%async_computation.4 | async-start | bytes 262144
  109.9 1.1 copy-start.1
  264.6 2.5 copy-start.7
  264.6 2.5 copy-start.11
  267.0 1.9 copy-start.8
  267.1 2.1 copy-start.13
  273.9 20.2 %all-to-all-start.3 = ((bf16[4,66,2048]{2,1,0:T(8,128)(2,1)}), bf16[4,66,2048]{2,1,0:T(8,128)(2,1)}, u32[]{:S(2)}, u32[]{:S(2)}) async-start(bf16[4,66,2048]{2,1,0:T(8,128)(2,1)} %reshape.269), calls=%async_computation.3 | async-start | bytes 2359296 | tf_op jit(solution)/shard_map/all_to_all | solution.py:169
Sparse Core Ops, SparseCore 0:
  150.4 70.9 all-reduce.4
where the time goes:
time: 318 us; the launch traced here: 316 us
  waiting for transfers between devices  96.5 us (30%)
  blocking collectives  82.8 us (26%)
  local copies, waits for them, and re-layouts  65.5 us (21%)
  other arithmetic  24 us (8%)
  between operations  21.5 us (7%)
  matrix products  13.2 us (4%)
  starting transfers between devices  13.1 us (4%)
    unnamed x2, waiting for transfers between devices  70.5 us
    all_gather x1, blocking collectives, shards(): lax.all_gather(teacher_p_half, 'dp', axis=0, tiled=True)  31.9 us
    all_gather x1, blocking collectives, shards(): lax.all_gather(passage_half, 'dp', axis=0, tiled=True)  30.7 us
    all_to_all x1, blocking collectives, shards(): lax.all_to_all(send_grads, 'expert', split_axis=0, concat_axis=0, tiled=T...  20.2 us
    all_to_all x1, waiting for transfers between devices, shards(): lax.all_to_all(send_rows, 'expert', split_axis=0, concat_axis=0, tiled=True)  14.4 us
    all_to_all x1, waiting for transfers between devices, shards(): lax.all_to_all(row_grad.reshape(group_size, capacity, model_width), 'expe...  11.6 us
    gather x2, local copies, waits for them, and re-layouts, shards(): back_grad.reshape(slot_total, model_width)[slot_index].astype(jnp.float32)  7.27 us
    dot_general x5, matrix products, contract_last(): lax.dot_general(left_mat, right_mat, (((1,), (1,)), ((), ())), preferred_...  6.63 us
  transfers between devices with their start and end apart: 4, of which 3 were waited for; matrix products, arithmetic and copies ran while one was open for 1% of the time, Pallas kernels for 0%

commit v1 on v0

v1 whole, which is shorter than its diff:
```python
import functools

import jax
import jax.numpy as jnp
from jax import lax
from jax.experimental import pallas as pl
from jax.experimental.pallas import tpu as pltpu
from jax.sharding import PartitionSpec as P

QLEN = 32
PLEN = 48
student_scale = 50.0
teacher_scale = 80.0
loss_scale = 64.0
norm_eps = 1e-06
MESH = pl.DeviceIdType.MESH
F32 = jnp.float32
BF16 = jnp.bfloat16
LANES = 128


def mm(left, right):
    return jnp.dot(left, right, preferred_element_type=F32)


def mm_last(left, right):
    return lax.dot_general(left, right, (((1,), (1,)), ((), ())), preferred_element_type=F32)


def iota(shape, dim):
    return lax.broadcasted_iota(jnp.int32, shape, dim)


def unit_rows(values):
    inverse = lax.rsqrt(jnp.sum(values * values, axis=-1, keepdims=True) + norm_eps)
    return values * inverse, inverse


def kernel(
    dims,
    tok_ref, wg_hbm, wu_hbm, wd_hbm, ids_ref, probs_ref, tq_ref, tp_ref, pos_ref,
    moe_ref, tgrad_ref, ggrad_ref, loss_ref,
    xbuf, wg, wu, wd, c1, c2, hid, meta, wf, wt,
    cbuf, crecv, slab, tmine, smine, tgath, sgath, tmat, smat, unit_buf,
    ogmine, ogbuf, ogmat, hgpad, ggsend, ggrecv,
    s_a, r_a, s_b, r_b, s_c, r_c, keep0, keep2,
    send_sem, recv_sem, t_send, t_recv, s_send, s_recv, loc_sem,
):
    dp, ex, rows, width, ff, nq, npas, rp, tok_chunks, col_chunks = dims
    me = lax.axis_index("dp")
    my_e = lax.axis_index("expert")
    half = ex // 2
    sib = my_e + 1 - 2 * lax.rem(my_e, 2)
    cross = lax.rem(my_e + half, ex)
    xsib = lax.rem(sib + half, ex)
    peers = [None, sib, cross, xsib]
    chunk_rows = rows // tok_chunks
    dc = width // col_chunks
    counter = [0]
    started = []

    def remote(src, dst, target):
        at = counter[0]
        counter[0] += 1
        copy = pltpu.make_async_remote_copy(
            src_ref=src, dst_ref=dst, send_sem=send_sem.at[at], recv_sem=recv_sem.at[at],
            device_id=(me, target), device_id_type=MESH,
        )
        started.append(copy)
        return copy

    loads = [
        pltpu.make_async_copy(tok_ref, xbuf.at[pl.ds(0, rows)], loc_sem.at[0]),
        pltpu.make_async_copy(wg_hbm.at[0], wg, loc_sem.at[1]),
        pltpu.make_async_copy(wu_hbm.at[0], wu, loc_sem.at[2]),
        pltpu.make_async_copy(wd_hbm.at[0], wd, loc_sem.at[3]),
    ]
    for load in loads:
        load.start()

    barrier = pltpu.get_barrier_semaphore()
    for peer in peers[1:]:
        pl.semaphore_signal(barrier, inc=1, device_id=(me, peer), device_id_type=MESH)

    def greet(off, carry):
        pl.semaphore_signal(
            barrier, inc=1, device_id=(lax.rem(me + off, dp), my_e), device_id_type=MESH
        )
        return carry

    lax.fori_loop(1, dp, greet, 0)

    ids = ids_ref[...]
    probs = probs_ref[...].astype(F32)
    lane = iota((rows, LANES), 1)
    spread = jnp.zeros((rows, LANES), F32)
    for k in range(ids.shape[1]):
        spread += jnp.where(lane == ids[:, k : k + 1], probs[:, k : k + 1], 0.0)
    meta[0] = jnp.transpose(spread)[:8]

    slab[...] = jnp.zeros_like(slab)
    slab[0:nq, :] = unit_rows(tq_ref[0].astype(F32))[0]
    slab[nq : nq + npas, :] = unit_rows(tp_ref[0].astype(F32))[0]
    lane_row = iota((1, LANES), 1)
    pos_row = jnp.zeros((1, LANES), F32)
    for q in range(nq):
        value = pos_ref[0:1, q : q + 1]
        pos_row += jnp.where(lane_row == 2 * q, (value >> 6).astype(F32), 0.0)
        pos_row += jnp.where(lane_row == 2 * q + 1, (value & 63).astype(F32), 0.0)
    slab[nq + npas : nq + npas + 1, 0:LANES] = pos_row
    tmine[...] = slab[...].astype(BF16)

    pl.semaphore_wait(barrier, ex - 1 + dp - 1)

    token_copies = []
    for k in range(tok_chunks):
        at = pl.ds(k * chunk_rows, chunk_rows)
        to = pl.ds(2 * rows + k * chunk_rows, chunk_rows)
        token_copies.append(remote(tok_ref.at[at], xbuf.at[to], cross))
    sib_copy = remote(tok_ref, xbuf.at[pl.ds(rows, rows)], sib)
    meta_copies = [remote(meta.at[0], meta.at[s], peers[s]) for s in range(1, ex)]
    token_copies[0].start()
    sib_copy.start()
    for copy in meta_copies:
        copy.start()
    for copy in token_copies[1:]:
        copy.start()

    def spread_copy(off, src, gath, s_sem, r_sem, incoming):
        slot = lax.rem(me + dp - off, dp) if incoming else me
        return pltpu.make_async_remote_copy(
            src_ref=src, dst_ref=gath.at[slot], send_sem=s_sem.at[off], recv_sem=r_sem.at[off],
            device_id=(lax.rem(me + off, dp), my_e), device_id_type=MESH,
        )

    def spread_start(src, gath, s_sem, r_sem):
        def body(off, carry):
            spread_copy(off, src, gath, s_sem, r_sem, False).start()
            return carry

        lax.fori_loop(1, dp, body, 0)
        gath[me] = src[...]

    def spread_wait(src, gath, s_sem, r_sem):
        def body(off, carry):
            spread_copy(off, src, gath, s_sem, r_sem, True).wait_recv()
            return carry

        lax.fori_loop(1, dp, body, 0)

    def spread_done(src, gath, s_sem, r_sem):
        def body(off, carry):
            spread_copy(off, src, gath, s_sem, r_sem, False).wait_send()
            return carry

        lax.fori_loop(1, dp, body, 0)

    spread_start(tmine, tgath, t_send, t_recv)

    tile = 256 if ff % 256 == 0 else ff

    def forward(start, count):
        at = pl.ds(start, count)

        def body(i, carry):
            cols = pl.ds(pl.multiple_of(i * tile, tile), tile)
            values = xbuf[at, :]
            gate = mm(values, wg[:, cols])
            up = mm(values, wu[:, cols])
            sig = 1.0 / (1.0 + jnp.exp(-gate))
            act = gate * sig
            hid[at, cols] = (act * up).astype(BF16)
            c2[at, cols] = act
            c1[at, cols] = up * (sig * (1.0 + gate * (1.0 - sig)))
            return carry

        lax.fori_loop(0, ff // tile, body, 0)

    loads[0].wait()
    loads[1].wait()
    loads[2].wait()
    sib_copy.wait_recv()
    forward(0, 2 * rows)
    forward_copies = []
    for k in range(tok_chunks):
        token_copies[k].wait_recv()
        at = pl.ds(2 * rows + k * chunk_rows, chunk_rows)
        to = pl.ds(3 * rows + k * chunk_rows, chunk_rows)
        copy = remote(xbuf.at[at], xbuf.at[to], sib)
        copy.start()
        forward_copies.append(copy)

    for copy in meta_copies:
        copy.wait_recv()
    t_at = iota((rp, rows), 1)
    segment = jnp.where(t_at < nq * QLEN, t_at // QLEN, nq + (t_at - nq * QLEN) // PLEN)
    member = segment == iota((rp, rows), 0)
    wf[...] = jnp.zeros_like(wf)
    for s in range(ex):
        prow = jnp.sum(jnp.where(iota((8, rows), 0) == my_e, meta[s], 0.0), axis=0, keepdims=True)
        wf[s * rp : (s + 1) * rp, s * rows : (s + 1) * rows] = jnp.where(member, prow, 0.0)
    for s in range(ex):
        wt[s * rows : (s + 1) * rows, :] = jnp.transpose(wf[:, s * rows : (s + 1) * rows])
    loads[3].wait()

    for copy in forward_copies:
        copy.wait_recv()
    forward(2 * rows, 2 * rows)

    nseg = ex * rp
    pooled_hid = mm(wf[0:nseg, :].astype(BF16), hid[...])
    high = pooled_hid.astype(BF16)
    low = (pooled_hid - high.astype(F32)).astype(BF16)

    def pooled_cols(j, carry):
        cols = pl.ds(pl.multiple_of(j * dc, dc), dc)
        part = mm(high, wd[:, cols]) + mm(low, wd[:, cols])
        for s in range(ex):
            cbuf[s, :, cols] = part[s * rp : (s + 1) * rp, :]
        return carry

    lax.fori_loop(0, col_chunks, pooled_cols, 0)
    pooled_copies = [remote(cbuf.at[s], crecv.at[s], peers[s]) for s in range(1, ex)]
    for s in (2, 3, 1):
        pooled_copies[s - 1].start()

    pcol = jnp.sum(wt[...], axis=1, keepdims=True)

    def moe_cols(j, carry):
        cols = pl.ds(pl.multiple_of(j * dc, dc), dc)
        part = mm(hid[...], wd[:, cols]) * pcol
        keep0[0, j] = part[0:rows]
        s_c[0, j] = part[rows : 2 * rows].astype(BF16)
        keep2[j] = part[2 * rows : 3 * rows]
        s_a[0, j] = part[3 * rows :].astype(BF16)
        return carry

    lax.fori_loop(0, col_chunks, moe_cols, 0)
    moe_a = remote(s_a.at[0], r_a.at[0], sib)
    moe_c = remote(s_c.at[0], r_c.at[0], sib)
    moe_a.start()

    for copy in pooled_copies:
        copy.wait_recv()
    row_at = iota((rp, 1), 0)
    is_query = row_at < nq
    total = cbuf[0] + crecv[1] + crecv[2] + crecv[3]
    pooled = total * jnp.where(is_query, 1.0 / QLEN, 1.0 / PLEN)
    units, inverse = unit_rows(pooled)
    unit_buf[...] = units
    smine[...] = units.astype(BF16)
    spread_start(smine, sgath, s_send, s_recv)

    moe_c.start()
    moe_a.wait_recv()
    for j in range(col_chunks):
        s_b[0, j] = (keep2[j] + r_a[0, j].astype(F32)).astype(BF16)
    moe_b = [remote(s_b.at[0, j], r_b.at[0, j], cross) for j in range(col_chunks)]
    for copy in moe_b[: col_chunks // 2]:
        copy.start()

    spread_wait(tmine, tgath, t_send, t_recv)
    for i in range(dp):
        tmat[i * rp : (i + 1) * rp, :] = tgath[i].astype(F32)
    tall = tmat[...].astype(BF16)
    teacher = teacher_scale * mm_last(tall, tall)
    n = dp * rp
    row = iota((n, n), 0)
    col = iota((n, n), 1)
    col_in = col % rp
    is_row = (row % rp) < nq
    is_pass = jnp.logical_and(col_in >= nq, col_in < nq + npas)
    live = jnp.logical_and(is_row, is_pass)
    pad_row = jnp.where(col == (row // rp) * rp + nq + npas, 1.0, 0.0).astype(BF16)
    codes = mm(pad_row, tall[:, 0:LANES])
    code_lane = iota((n, LANES), 1)
    code_at = 2 * (iota((n, LANES), 0) % rp)
    positive = jnp.sum(
        jnp.where(code_lane == code_at, codes * 64.0, 0.0)
        + jnp.where(code_lane == code_at + 1, codes, 0.0),
        axis=1,
        keepdims=True,
    ).astype(jnp.int32)
    is_pos = jnp.logical_and(live, ((col // rp) * npas + col_in - nq) == positive)
    teacher = jnp.where(live, teacher, 0.0)
    teacher_exp = jnp.where(live, jnp.exp(teacher), 0.0)
    teacher_total = jnp.sum(teacher_exp, axis=1, keepdims=True)
    row_live = (iota((n, 1), 0) % rp) < nq
    teacher_total = jnp.where(row_live, teacher_total, 1.0)

    spread_wait(smine, sgath, s_send, s_recv)
    for i in range(dp):
        smat[i * rp : (i + 1) * rp, :] = sgath[i].astype(F32)
    sall = smat[...].astype(BF16)
    student = jnp.where(live, student_scale * mm_last(sall, sall), 0.0)
    student_exp = jnp.where(live, jnp.exp(student), 0.0)
    student_total = jnp.where(row_live, jnp.sum(student_exp, axis=1, keepdims=True), 1.0)
    crossed = jnp.sum(teacher_exp * (teacher - student), axis=1, keepdims=True)
    pos_score = jnp.sum(jnp.where(is_pos, student, 0.0), axis=1, keepdims=True)
    loss = (
        2.0 * jnp.log(student_total) - pos_score + crossed / teacher_total - jnp.log(teacher_total)
    )
    coeffs = (
        2.0 * student_exp / student_total
        - teacher_exp / teacher_total
        - jnp.where(is_pos, 1.0, 0.0)
    ).astype(BF16)
    pick = jnp.where(iota((8, n), 1) == me * rp + iota((8, n), 0), 1.0, 0.0)
    pick = jnp.where(iota((8, n), 0) < rp, pick, 0.0).astype(BF16)
    mine = mm(pick, coeffs) + mm_last(pick, coeffs)
    unit_grad = (student_scale * mm(mine.astype(BF16), sall))[0:rp]
    for q in range(nq):
        chosen = jnp.where(iota((n, 1), 0) == me * rp + q, loss, 0.0)
        loss_ref[0:1, q : q + 1] = jnp.sum(chosen, axis=0, keepdims=True)
    units = unit_buf[...]
    grad = inverse * (unit_grad - units * jnp.sum(units * unit_grad, axis=-1, keepdims=True))
    grad = grad * jnp.where(is_query, loss_scale / QLEN, loss_scale / PLEN)
    ogmine[...] = grad.astype(BF16)
    og_copies = [remote(ogmine, ogbuf.at[s], peers[s]) for s in range(1, ex)]
    for s in (2, 3, 1):
        og_copies[s - 1].start()
    for copy in moe_b[col_chunks // 2 :]:
        copy.start()

    hgpad[...] = jnp.zeros_like(hgpad)
    ogmat[0:rp, :] = grad
    for s in (1, 3, 2):
        og_copies[s - 1].wait_recv()
    for s in range(1, ex):
        ogmat[s * rp : (s + 1) * rp, :] = ogbuf[s].astype(F32)
    hg = mm_last(ogmat[...].astype(BF16), wd[...]).astype(BF16)
    hgpad[0:nseg, :] = hg
    gpart = c1
    upart = c2

    def back_rows(start, count):
        at = pl.ds(start, count)
        hidden_grad = mm(wt[at, :].astype(BF16), hgpad[...])
        gate_part = (hidden_grad * gpart[at, :]).astype(BF16)
        up_part = (hidden_grad * upart[at, :]).astype(BF16)
        return gate_part, up_part

    tg_a = [remote(s_a.at[1, j], r_a.at[1, j], sib) for j in range(col_chunks)]
    tg_b = [remote(s_b.at[1, j], r_b.at[1, j], cross) for j in range(col_chunks)]
    tg_c = [remote(s_c.at[1, j], r_c.at[1, j], sib) for j in range(col_chunks)]

    def combine(j):
        tg_a[j].wait_recv()
        s_b[1, j] = (keep2[j] + r_a[1, j].astype(F32)).astype(BF16)
        tg_b[j].start()

    gate_part, up_part = back_rows(2 * rows, 2 * rows)
    for j in range(col_chunks):
        at = pl.ds(j * dc, dc)
        part = mm_last(gate_part, wg[at, :]) + mm_last(up_part, wu[at, :])
        keep2[j] = part[0:rows]
        s_a[1, j] = part[rows:].astype(BF16)
        tg_a[j].start()
        if j:
            combine(j - 1)
    combine(col_chunks - 1)

    scores = mm_last(hg, hid[...])
    gg_copies = [remote(ggsend.at[s], ggrecv.at[s], peers[s]) for s in range(1, ex)]
    for s in range(ex):
        part = scores[s * rp : (s + 1) * rp, s * rows : (s + 1) * rows]
        line = jnp.sum(jnp.where(member, part, 0.0), axis=0, keepdims=True)
        ggsend[s] = jnp.where(iota((8, rows), 0) == my_e, line, 0.0)
    for copy in gg_copies:
        copy.start()

    gate_part, up_part = back_rows(0, 2 * rows)
    for j in range(col_chunks):
        at = pl.ds(j * dc, dc)
        part = mm_last(gate_part, wg[at, :]) + mm_last(up_part, wu[at, :])
        keep0[1, j] = part[0:rows]
        s_c[1, j] = part[rows:].astype(BF16)
        tg_c[j].start()

    moe_c.wait_recv()
    for j in range(col_chunks):
        moe_b[j].wait_recv()
        total = keep0[0, j] + r_c[0, j].astype(F32) + r_b[0, j].astype(F32)
        moe_ref[:, j * dc : (j + 1) * dc] = total.astype(BF16)
    for copy in gg_copies:
        copy.wait_recv()
    table = ggsend[0] + ggrecv[1] + ggrecv[2] + ggrecv[3]
    wf[0:8, 0:rows] = table
    table = jnp.transpose(wf[:, 0:rows])
    ids = ids_ref[...]
    for k in range(ids.shape[1]):
        chosen = jnp.where(lane == ids[:, k : k + 1], table, 0.0)
        ggrad_ref[:, k : k + 1] = jnp.sum(chosen, axis=1, keepdims=True)
    for j in range(col_chunks):
        tg_c[j].wait_recv()
        tg_b[j].wait_recv()
        total = keep0[1, j] + r_c[1, j].astype(F32) + r_b[1, j].astype(F32)
        tgrad_ref[:, j * dc : (j + 1) * dc] = total.astype(BF16)

    for copy in started:
        copy.wait_send()
    spread_done(tmine, tgath, t_send, t_recv)
    spread_done(smine, sgath, s_send, s_recv)


def shards(
    dp, ex,
    tokens, expert_ids, gate_probs, w_gate, w_up, w_down, teacher_queries, teacher_passages, positives,
):
    rows, width = tokens.shape
    ff = w_gate.shape[2]
    nq = teacher_queries.shape[1]
    npas = teacher_passages.shape[1]
    rp = -(-(nq + npas + 1) // 4) * 4
    tok_chunks, col_chunks = 4, 4
    dc = width // col_chunks
    dims = (dp, ex, rows, width, ff, nq, npas, rp, tok_chunks, col_chunks)
    copies = 2 * tok_chunks + 1 + 4 * (ex - 1) + 2 + col_chunks + 3 * col_chunks
    vmem = pl.BlockSpec(memory_space=pltpu.VMEM)
    hbm = pl.BlockSpec(memory_space=pl.ANY)
    dma = pltpu.SemaphoreType.DMA
    moved = pltpu.VMEM((2, col_chunks, rows, dc), BF16)
    moe, tgrad, ggrad, loss = pl.pallas_call(
        functools.partial(kernel, dims),
        out_shape=(
            jax.ShapeDtypeStruct((rows, width), BF16),
            jax.ShapeDtypeStruct((rows, width), BF16),
            jax.ShapeDtypeStruct(expert_ids.shape, F32),
            jax.ShapeDtypeStruct((1, nq), F32),
        ),
        in_specs=[hbm] * 4 + [vmem] * 5,
        out_specs=(vmem,) * 4,
        scratch_shapes=[
            pltpu.VMEM((ex * rows, width), BF16),
            pltpu.VMEM((width, ff), BF16),
            pltpu.VMEM((width, ff), BF16),
            pltpu.VMEM((ff, width), BF16),
            pltpu.VMEM((ex * rows, ff), F32),
            pltpu.VMEM((ex * rows, ff), F32),
            pltpu.VMEM((ex * rows, ff), BF16),
            pltpu.VMEM((ex, 8, rows), F32),
            pltpu.VMEM((LANES, ex * rows), F32),
            pltpu.VMEM((ex * rows, LANES), F32),
            pltpu.VMEM((ex, rp, width), F32),
            pltpu.VMEM((ex, rp, width), F32),
            pltpu.VMEM((rp, width), F32),
            pltpu.VMEM((rp, width), BF16),
            pltpu.VMEM((rp, width), BF16),
            pltpu.VMEM((dp, rp, width), BF16),
            pltpu.VMEM((dp, rp, width), BF16),
            pltpu.VMEM((dp * rp, width), F32),
            pltpu.VMEM((dp * rp, width), F32),
            pltpu.VMEM((rp, width), F32),
            pltpu.VMEM((rp, width), BF16),
            pltpu.VMEM((ex, rp, width), BF16),
            pltpu.VMEM((ex * rp, width), F32),
            pltpu.VMEM((LANES, ff), BF16),
            pltpu.VMEM((ex, 8, rows), F32),
            pltpu.VMEM((ex, 8, rows), F32),
            moved, moved, moved, moved, moved, moved,
            pltpu.VMEM((2, col_chunks, rows, dc), F32),
            pltpu.VMEM((col_chunks, rows, dc), F32),
            dma((copies,)), dma((copies,)),
            dma((dp,)), dma((dp,)), dma((dp,)), dma((dp,)),
            dma((4,)),
        ],
        compiler_params=pltpu.CompilerParams(
            collective_id=0, has_side_effects=True, vmem_limit_bytes=60 * 1024 * 1024
        ),
    )(
        tokens, w_gate, w_up, w_down, expert_ids, gate_probs,
        teacher_queries, teacher_passages, positives,
    )
    return moe, tgrad, ggrad, loss


def solution(mesh):
    in_specs = (
        P(("dp", "expert"), None),
        P(("dp", "expert"), None),
        P(("dp", "expert"), None),
        P("expert", None, None),
        P("expert", None, None),
        P("expert", None, None),
        P("expert", "dp", None),
        P("expert", "dp", None),
        P("expert", "dp"),
    )
    out_specs = (
        P(("dp", "expert"), None),
        P(("dp", "expert"), None),
        P(("dp", "expert"), None),
        P("expert", "dp"),
    )
    body = functools.partial(shards, mesh.shape["dp"], mesh.shape["expert"])
    return jax.shard_map(body, mesh=mesh, in_specs=in_specs, out_specs=out_specs, check_vma=False)
```

time: 318 us -> 69 us (0.22)
  waiting for transfers between devices: 96.5 us -> 0 us
  blocking collectives: 82.8 us -> 0 us
  Pallas kernels: 0 us -> 57.5 us
  local copies, waits for them, and re-layouts: 65.5 us -> 8.03 us
  other arithmetic: 24 us -> 0 us
  between operations: 21.5 us -> 3.1 us
  matrix products: 13.2 us -> 0 us
  starting transfers between devices: 13.1 us -> 0 us
    unnamed x2 -> x0, waiting for transfers between devices: 70.5 us -> none
    all_gather x2 -> x0, blocking collectives: 62.6 us -> none  [the longest x1 31.9 us: shards(): lax.all_gather(teacher_p_half, 'dp', axis=0, tiled=True)]
    pallas_call x0 -> x1, Pallas kernels: none -> 57.5 us  [shards(): pl.pallas_call(functools.partial(kernel, dims), out_shape=(jax.ShapeDtype...]
    all_to_all x3 -> x0, waiting for transfers between devices: 26 us -> none  [the longest x1 14.4 us: shards(): lax.all_to_all(send_rows, 'expert', split_axis=0, concat_axis=0, tiled=True)]
    reshape x10 -> x0, local copies, waits for them, and re-layouts: 24.4 us -> none  [the longest x1 3.71 us: shards(): grad_rep = jnp.repeat(out_grad, top_count, axis=0)]
    gather x5 -> x0, local copies, waits for them, and re-layouts: 24.2 us -> none  [the longest x2 7.27 us: shards(): back_grad.reshape(slot_total, model_width)[slot_index].astype(jnp.float32)]
    all_to_all x1 -> x0, blocking collectives: 20.2 us -> none  [shards(): lax.all_to_all(send_grads, 'expert', split_axis=0, concat_axis=0, tiled=T...]
    reduce_sum x12 -> x0, other arithmetic: 16.9 us -> none  [the longest x1 4.79 us: shards(): jnp.sum((gate_flat * token_out).reshape(tok_rows, top_count, model_width)...]
  transfers between devices with their start and end apart: 4 -> 0, of which waited for: 3 -> 0; matrix products, arithmetic and copies ran while one was open for 1% -> 0% of each run, Pallas kernels for 0% -> 0%
where the time goes in v1:
time: 69 us; the launch traced here: 68.6 us
  Pallas kernels  57.5 us (83%)
  local copies, waits for them, and re-layouts  8.03 us (12%)
  between operations  3.1 us (4%)
    pallas_call x1, Pallas kernels, shards(): pl.pallas_call(functools.partial(kernel, dims), out_shape=(jax.ShapeDtype...  57.5 us
    unnamed x4, local copies, waits for them, and re-layouts  6.56 us
    pallas_call x1, local copies, waits for them, and re-layouts, shards(): pl.pallas_call(functools.partial(kernel, dims), out_shape=(jax.ShapeDtype...  1.48 us

profile of v1, /device:TPU:0, one launch (start us, length us, event | category | flops | bytes accessed | tf_op | source)
XLA Modules:
  0.0 68.6 jit_solution(12810667895799136898)
XLA Ops:
  1.3 1.4 %copy.14.probs_ref = bf16[128,2]{1,0:T(8,128)(2,1)} copy(bf16[128,2]{0,1:T(2,128)(2,1)} %param.11) | data formatting | bytes 1024 | tf_op args[2]
  2.7 1.4 %copy.13.ids_ref = s32[128,2]{1,0:T(8,128)} copy(s32[128,2]{0,1:T(2,128)} %param.10) | data formatting | bytes 2048 | tf_op args[1]
  4.1 57.5 %shard_map.120 = (bf16[128,2048]{1,0:T(8,128)(2,1)}, bf16[128,2048]{1,0:T(8,128)(2,1)}, f32[128,2]{1,0:T(8,128)}, f32[1,1]{1,0:T(1,128)}) custom-call(bf16[128,2048]{1,0:T(8,128)(2,1)} %tok_ref.1, bf16[1,2048,768]{2,1,0:T(8,128)(2,1)} %wg_hbm.1, bf16[1,2048,768]{2,1,0:T(8,128)(2,1)} %wu_hbm.1, bf16[1,768,2048]{2,1,0:T(8,128)(2,1)} %wd_hbm.1, ...), custom_call_target="tpu_custom_call" | custom-call | tf_op jit(solution)/shard_map/pallas_call | solution.py:423
  61.6 1.5 %copy.15 = f32[128,2]{0,1:T(2,128)} copy(f32[128,2]{1,0:T(8,128)} %get-tuple-element.6) | data formatting | bytes 2048 | tf_op jit(solution)/shard_map/pallas_call | solution.py:423
  63.1 1.9 %copy.20 = bf16[128,2048]{1,0:T(8,128)(2,1)} copy(bf16[128,2048]{1,0:T(8,128)(2,1)} %get-tuple-element.12) | data formatting | bytes 1048576
  65.0 1.9 %copy.21 = bf16[128,2048]{1,0:T(8,128)(2,1)} copy(bf16[128,2048]{1,0:T(8,128)(2,1)} %get-tuple-element.13) | data formatting | bytes 1048576

commit v2 on v1

--- a/solution.py
+++ b/solution.py
@@ -44,7 +44,7 @@
     cbuf, crecv, slab, tmine, smine, tgath, sgath, tmat, smat, unit_buf,
     ogmine, ogbuf, ogmat, hgpad, ggsend, ggrecv,
     s_a, r_a, s_b, r_b, s_c, r_c, keep0, keep2,
-    send_sem, recv_sem, t_send, t_recv, s_send, s_recv, loc_sem,
+    out_v, send_sem, recv_sem, t_send, t_recv, s_send, s_recv, loc_sem, out_sem,
 ):
     dp, ex, rows, width, ff, nq, npas, rp, tok_chunks, col_chunks = dims
     me = lax.axis_index("dp")
@@ -55,6 +55,18 @@
     xsib = lax.rem(sib + half, ex)
     peers = [None, sib, cross, xsib]
     chunk_rows = rows // tok_chunks
+    part_rows = rows // 2
+    places = [
+        [(0, rows, 0)],
+        [(rows, rows, 0)],
+        [(2 * rows, part_rows, 0), (3 * rows, part_rows, part_rows)],
+        [(2 * rows + part_rows, part_rows, 0), (3 * rows + part_rows, part_rows, part_rows)],
+    ]
+
+    def far(slot, k):
+        token = k * chunk_rows
+        return 2 * rows + (token // part_rows) * rows + (slot - 2) * part_rows + token % part_rows
+
     dc = width // col_chunks
     counter = [0]
     started = []
@@ -92,11 +104,11 @@
 
     ids = ids_ref[...]
     probs = probs_ref[...].astype(F32)
-    lane = iota((rows, LANES), 1)
-    spread = jnp.zeros((rows, LANES), F32)
-    for k in range(ids.shape[1]):
-        spread += jnp.where(lane == ids[:, k : k + 1], probs[:, k : k + 1], 0.0)
-    meta[0] = jnp.transpose(spread)[:8]
+    lane = iota((8, rows), 0)
+    spread = jnp.zeros((8, rows), F32)
+    for k in range(ids.shape[0]):
+        spread += jnp.where(lane == ids[k : k + 1, :], probs[k : k + 1, :], 0.0)
+    meta[0] = spread
 
     slab[...] = jnp.zeros_like(slab)
     slab[0:nq, :] = unit_rows(tq_ref[0].astype(F32))[0]
@@ -115,7 +127,7 @@
     token_copies = []
     for k in range(tok_chunks):
         at = pl.ds(k * chunk_rows, chunk_rows)
-        to = pl.ds(2 * rows + k * chunk_rows, chunk_rows)
+        to = pl.ds(far(2, k), chunk_rows)
         token_copies.append(remote(tok_ref.at[at], xbuf.at[to], cross))
     sib_copy = remote(tok_ref, xbuf.at[pl.ds(rows, rows)], sib)
     meta_copies = [remote(meta.at[0], meta.at[s], peers[s]) for s in range(1, ex)]
@@ -184,11 +196,15 @@
     forward_copies = []
     for k in range(tok_chunks):
         token_copies[k].wait_recv()
-        at = pl.ds(2 * rows + k * chunk_rows, chunk_rows)
-        to = pl.ds(3 * rows + k * chunk_rows, chunk_rows)
-        copy = remote(xbuf.at[at], xbuf.at[to], sib)
+        copy = remote(
+            xbuf.at[pl.ds(far(2, k), chunk_rows)], xbuf.at[pl.ds(far(3, k), chunk_rows)], sib
+        )
         copy.start()
         forward_copies.append(copy)
+        if k == tok_chunks // 2 - 1:
+            for copy in forward_copies:
+                copy.wait_recv()
+            forward(2 * rows, rows)
 
     for copy in meta_copies:
         copy.wait_recv()
@@ -198,25 +214,29 @@
     wf[...] = jnp.zeros_like(wf)
     for s in range(ex):
         prow = jnp.sum(jnp.where(iota((8, rows), 0) == my_e, meta[s], 0.0), axis=0, keepdims=True)
-        wf[s * rp : (s + 1) * rp, s * rows : (s + 1) * rows] = jnp.where(member, prow, 0.0)
+        weights = jnp.where(member, prow, 0.0)
+        for start, count, token in places[s]:
+            wf[s * rp : (s + 1) * rp, start : start + count] = weights[:, token : token + count]
     for s in range(ex):
         wt[s * rows : (s + 1) * rows, :] = jnp.transpose(wf[:, s * rows : (s + 1) * rows])
     loads[3].wait()
 
-    for copy in forward_copies:
+    for copy in forward_copies[tok_chunks // 2 :]:
         copy.wait_recv()
-    forward(2 * rows, 2 * rows)
+    forward(3 * rows, rows)
 
     nseg = ex * rp
     pooled_hid = mm(wf[0:nseg, :].astype(BF16), hid[...])
     high = pooled_hid.astype(BF16)
     low = (pooled_hid - high.astype(F32)).astype(BF16)
+    both = jnp.concatenate([high, low], axis=0)
 
     def pooled_cols(j, carry):
         cols = pl.ds(pl.multiple_of(j * dc, dc), dc)
-        part = mm(high, wd[:, cols]) + mm(low, wd[:, cols])
+        part = mm(both, wd[:, cols])
+        part = part[0:nseg] + part[nseg:]
         for s in range(ex):
-            cbuf[s, :, cols] = part[s * rp : (s + 1) * rp, :]
+            cbuf[s, :, cols] = part[s * rp : (s + 1) * rp, :].astype(BF16)
         return carry
 
     lax.fori_loop(0, col_chunks, pooled_cols, 0)
@@ -226,38 +246,49 @@
 
     pcol = jnp.sum(wt[...], axis=1, keepdims=True)
 
-    def moe_cols(j, carry):
-        cols = pl.ds(pl.multiple_of(j * dc, dc), dc)
-        part = mm(hid[...], wd[:, cols]) * pcol
+    moe_a = [remote(s_a.at[0, j], r_a.at[0, j], sib) for j in range(col_chunks)]
+    moe_b = [remote(s_b.at[0, j], r_b.at[0, j], cross) for j in range(col_chunks)]
+    moe_c = remote(s_c.at[0], r_c.at[0], sib)
+
+    def moe_part(j):
+        part = mm(hid[...], wd[:, j * dc : (j + 1) * dc]) * pcol
         keep0[0, j] = part[0:rows]
         s_c[0, j] = part[rows : 2 * rows].astype(BF16)
-        keep2[j] = part[2 * rows : 3 * rows]
-        s_a[0, j] = part[3 * rows :].astype(BF16)
-        return carry
-
-    lax.fori_loop(0, col_chunks, moe_cols, 0)
-    moe_a = remote(s_a.at[0], r_a.at[0], sib)
-    moe_c = remote(s_c.at[0], r_c.at[0], sib)
-    moe_a.start()
+        for start, count, token in places[2]:
+            keep2[j, token : token + count] = part[start : start + count]
+        for start, count, token in places[3]:
+            s_a[0, j, token : token + count] = part[start : start + count].astype(BF16)
+        moe_a[j].start()
+
+    def moe_combine(j):
+        moe_a[j].wait_recv()
+        s_b[0, j] = (keep2[j] + r_a[0, j].astype(F32)).astype(BF16)
+
+    early = col_chunks // 2
+    for j in range(early + 1):
+        moe_part(j)
+        if j:
+            moe_combine(j - 1)
+            moe_b[j - 1].start()
 
     for copy in pooled_copies:
         copy.wait_recv()
     row_at = iota((rp, 1), 0)
     is_query = row_at < nq
-    total = cbuf[0] + crecv[1] + crecv[2] + crecv[3]
+    total = cbuf[0].astype(F32)
+    for s in range(1, ex):
+        total += crecv[s].astype(F32)
     pooled = total * jnp.where(is_query, 1.0 / QLEN, 1.0 / PLEN)
     units, inverse = unit_rows(pooled)
     unit_buf[...] = units
     smine[...] = units.astype(BF16)
     spread_start(smine, sgath, s_send, s_recv)
 
+    for j in range(early + 1, col_chunks):
+        moe_part(j)
     moe_c.start()
-    moe_a.wait_recv()
-    for j in range(col_chunks):
-        s_b[0, j] = (keep2[j] + r_a[0, j].astype(F32)).astype(BF16)
-    moe_b = [remote(s_b.at[0, j], r_b.at[0, j], cross) for j in range(col_chunks)]
-    for copy in moe_b[: col_chunks // 2]:
-        copy.start()
+    for j in range(early, col_chunks):
+        moe_combine(j)
 
     spread_wait(tmine, tgath, t_send, t_recv)
     for i in range(dp):
@@ -319,7 +350,7 @@
     og_copies = [remote(ogmine, ogbuf.at[s], peers[s]) for s in range(1, ex)]
     for s in (2, 3, 1):
         og_copies[s - 1].start()
-    for copy in moe_b[col_chunks // 2 :]:
+    for copy in moe_b[early:]:
         copy.start()
 
     hgpad[...] = jnp.zeros_like(hgpad)
@@ -353,8 +384,11 @@
     for j in range(col_chunks):
         at = pl.ds(j * dc, dc)
         part = mm_last(gate_part, wg[at, :]) + mm_last(up_part, wu[at, :])
-        keep2[j] = part[0:rows]
-        s_a[1, j] = part[rows:].astype(BF16)
+        for start, count, token in places[2]:
+            keep2[j, token : token + count] = part[start - 2 * rows : start - 2 * rows + count]
+        for start, count, token in places[3]:
+            shifted = part[start - 2 * rows : start - 2 * rows + count]
+            s_a[1, j, token : token + count] = shifted.astype(BF16)
         tg_a[j].start()
         if j:
             combine(j - 1)
@@ -363,7 +397,10 @@
     scores = mm_last(hg, hid[...])
     gg_copies = [remote(ggsend.at[s], ggrecv.at[s], peers[s]) for s in range(1, ex)]
     for s in range(ex):
-        part = scores[s * rp : (s + 1) * rp, s * rows : (s + 1) * rows]
+        part = jnp.concatenate(
+            [scores[s * rp : (s + 1) * rp, start : start + count] for start, count, _ in places[s]],
+            axis=1,
+        )
         line = jnp.sum(jnp.where(member, part, 0.0), axis=0, keepdims=True)
         ggsend[s] = jnp.where(iota((8, rows), 0) == my_e, line, 0.0)
     for copy in gg_copies:
@@ -377,30 +414,55 @@
         s_c[1, j] = part[rows:].astype(BF16)
         tg_c[j].start()
 
+    writes = []
+
+    def write(which, j, target):
+        cols = pl.ds(j * dc, dc)
+        copy = pltpu.make_async_copy(
+            out_v.at[which, :, cols], target.at[:, cols], out_sem.at[which, j]
+        )
+        copy.start()
+        writes.append(copy)
+
     moe_c.wait_recv()
     for j in range(col_chunks):
         moe_b[j].wait_recv()
         total = keep0[0, j] + r_c[0, j].astype(F32) + r_b[0, j].astype(F32)
-        moe_ref[:, j * dc : (j + 1) * dc] = total.astype(BF16)
+        out_v[0, :, j * dc : (j + 1) * dc] = total.astype(BF16)
+        write(0, j, moe_ref)
     for copy in gg_copies:
         copy.wait_recv()
     table = ggsend[0] + ggrecv[1] + ggrecv[2] + ggrecv[3]
-    wf[0:8, 0:rows] = table
-    table = jnp.transpose(wf[:, 0:rows])
     ids = ids_ref[...]
-    for k in range(ids.shape[1]):
-        chosen = jnp.where(lane == ids[:, k : k + 1], table, 0.0)
-        ggrad_ref[:, k : k + 1] = jnp.sum(chosen, axis=1, keepdims=True)
+    for k in range(ids.shape[0]):
+        chosen = jnp.where(lane == ids[k : k + 1, :], table, 0.0)
+        ggrad_ref[k : k + 1, :] = jnp.sum(chosen, axis=0, keepdims=True)
     for j in range(col_chunks):
         tg_c[j].wait_recv()
         tg_b[j].wait_recv()
         total = keep0[1, j] + r_c[1, j].astype(F32) + r_b[1, j].astype(F32)
-        tgrad_ref[:, j * dc : (j + 1) * dc] = total.astype(BF16)
+        out_v[1, :, j * dc : (j + 1) * dc] = total.astype(BF16)
+        write(1, j, tgrad_ref)
 
     for copy in started:
         copy.wait_send()
+    for copy in writes:
+        copy.wait()
     spread_done(tmine, tgath, t_send, t_recv)
     spread_done(smine, sgath, s_send, s_recv)
+
+
+def hand_on(moe_in, tgrad_in, ggrad_in, loss_in, moe, tgrad, ggrad, loss, sem):
+    copies = [
+        pltpu.make_async_copy(moe_in, moe, sem.at[0]),
+        pltpu.make_async_copy(tgrad_in, tgrad, sem.at[1]),
+    ]
+    for copy in copies:
+        copy.start()
+    ggrad[...] = ggrad_in[...]
+    loss[...] = loss_in[...]
+    for copy in copies:
+        copy.wait()
 
 
 def shards(
@@ -415,7 +477,7 @@
     tok_chunks, col_chunks = 4, 4
     dc = width // col_chunks
     dims = (dp, ex, rows, width, ff, nq, npas, rp, tok_chunks, col_chunks)
-    copies = 2 * tok_chunks + 1 + 4 * (ex - 1) + 2 + col_chunks + 3 * col_chunks
+    copies = 2 * tok_chunks + 1 + 4 * (ex - 1) + 1 + 2 * col_chunks + 3 * col_chunks
     vmem = pl.BlockSpec(memory_space=pltpu.VMEM)
     hbm = pl.BlockSpec(memory_space=pl.ANY)
     dma = pltpu.SemaphoreType.DMA
@@ -425,11 +487,11 @@
         out_shape=(
             jax.ShapeDtypeStruct((rows, width), BF16),
             jax.ShapeDtypeStruct((rows, width), BF16),
-            jax.ShapeDtypeStruct(expert_ids.shape, F32),
+            jax.ShapeDtypeStruct(expert_ids.shape[::-1], F32),
             jax.ShapeDtypeStruct((1, nq), F32),
         ),
         in_specs=[hbm] * 4 + [vmem] * 5,
-        out_specs=(vmem,) * 4,
+        out_specs=(hbm, hbm, vmem, vmem),
         scratch_shapes=[
             pltpu.VMEM((ex * rows, width), BF16),
             pltpu.VMEM((width, ff), BF16),
@@ -441,8 +503,8 @@
             pltpu.VMEM((ex, 8, rows), F32),
             pltpu.VMEM((LANES, ex * rows), F32),
             pltpu.VMEM((ex * rows, LANES), F32),
-            pltpu.VMEM((ex, rp, width), F32),
-            pltpu.VMEM((ex, rp, width), F32),
+            pltpu.VMEM((ex, rp, width), BF16),
+            pltpu.VMEM((ex, rp, width), BF16),
             pltpu.VMEM((rp, width), F32),
             pltpu.VMEM((rp, width), BF16),
             pltpu.VMEM((rp, width), BF16),
@@ -460,18 +522,27 @@
             moved, moved, moved, moved, moved, moved,
             pltpu.VMEM((2, col_chunks, rows, dc), F32),
             pltpu.VMEM((col_chunks, rows, dc), F32),
+            pltpu.VMEM((2, rows, width), BF16),
             dma((copies,)), dma((copies,)),
             dma((dp,)), dma((dp,)), dma((dp,)), dma((dp,)),
-            dma((4,)),
+            dma((4,)), dma((2, col_chunks)),
         ],
         compiler_params=pltpu.CompilerParams(
             collective_id=0, has_side_effects=True, vmem_limit_bytes=60 * 1024 * 1024
         ),
     )(
-        tokens, w_gate, w_up, w_down, expert_ids, gate_probs,
+        tokens, w_gate, w_up, w_down, expert_ids.T, gate_probs.T,
         teacher_queries, teacher_passages, positives,
     )
-    return moe, tgrad, ggrad, loss
+    moe, tgrad, ggrad, loss = pl.pallas_call(
+        hand_on,
+        out_shape=tuple(jax.ShapeDtypeStruct(a.shape, a.dtype) for a in (moe, tgrad, ggrad, loss)),
+        in_specs=[hbm, hbm, vmem, vmem],
+        out_specs=(hbm, hbm, vmem, vmem),
+        scratch_shapes=[dma((2,))],
+        compiler_params=pltpu.CompilerParams(vmem_limit_bytes=60 * 1024 * 1024),
+    )(moe, tgrad, ggrad, loss)
+    return moe, tgrad, ggrad.T, loss
 
 
 def solution(mesh):

time: 69 us -> 90 us (1.30)
  Pallas kernels: 57.5 us -> 88.5 us
  local copies, waits for them, and re-layouts: 8.03 us -> 0 us
  between operations: 3.1 us -> 1.29 us
    pallas_call x0 -> x1, Pallas kernels: none -> 34.7 us  [shards(): pl.pallas_call(hand_on, out_shape=tuple((jax.ShapeDtypeStruct(a.shape, a....]
    unnamed x4 -> x0, local copies, waits for them, and re-layouts: 6.56 us -> none
    pallas_call x1, Pallas kernels: 57.5 us -> 53.7 us  [shards(): pl.pallas_call(functools.partial(kernel, dims), out_shape=(jax.ShapeDtype...]
    pallas_call x1 -> x0, local copies, waits for them, and re-layouts: 1.48 us -> none  [shards(): pl.pallas_call(functools.partial(kernel, dims), out_shape=(jax.ShapeDtype...]
where the time goes in v2:
time: 90 us; the launch traced here: 89.8 us
  Pallas kernels  88.5 us (98%)
  between operations  1.29 us (1%)
    pallas_call x1, Pallas kernels, shards(): pl.pallas_call(functools.partial(kernel, dims), out_shape=(jax.ShapeDtype...  53.7 us
    pallas_call x1, Pallas kernels, shards(): pl.pallas_call(hand_on, out_shape=tuple((jax.ShapeDtypeStruct(a.shape, a....  34.7 us

profile of v2, /device:TPU:0, one launch (start us, length us, event | category | flops | bytes accessed | tf_op | source)
XLA Modules:
  0.0 89.8 jit_solution(5739603748067823130)
XLA Ops:
  1.3 53.7 %shard_map.120 = (bf16[128,2048]{1,0:T(8,128)(2,1)}, bf16[128,2048]{1,0:T(8,128)(2,1)}, f32[2,128]{1,0:T(2,128)}, f32[1,1]{1,0:T(1,128)}) custom-call(bf16[128,2048]{1,0:T(8,128)(2,1)} %tok_ref.1, bf16[1,2048,768]{2,1,0:T(8,128)(2,1)} %wg_hbm.1, bf16[1,2048,768]{2,1,0:T(8,128)(2,1)} %wu_hbm.1, bf16[1,768,2048]{2,1,0:T(8,128)(2,1)} %wd_hbm.1, ...), custom_call_target="tpu_custom_call" | custom-call | tf_op jit(solution)/shard_map/pallas_call | solution.py:485
  55.0 34.7 %shard_map.121 = (bf16[128,2048]{1,0:T(8,128)(2,1)}, bf16[128,2048]{1,0:T(8,128)(2,1)}, f32[2,128]{1,0:T(2,128)}, f32[1,1]{1,0:T(1,128)}) custom-call(bf16[128,2048]{1,0:T(8,128)(2,1)} %get-tuple-element.12.moe_in, bf16[128,2048]{1,0:T(8,128)(2,1)} %get-tuple-element.13.tgrad_in, f32[2,128]{1,0:T(2,128)} %get-tuple-element.14.ggrad_in, ...), custom_call_target="tpu_custom_call" | custom-call | tf_op jit(solution)/shard_map/pallas_call | solution.py:537

commit v3 on v2

--- a/solution.py
+++ b/solution.py
@@ -265,11 +265,8 @@
         s_b[0, j] = (keep2[j] + r_a[0, j].astype(F32)).astype(BF16)
 
     early = col_chunks // 2
-    for j in range(early + 1):
+    for j in range(early):
         moe_part(j)
-        if j:
-            moe_combine(j - 1)
-            moe_b[j - 1].start()
 
     for copy in pooled_copies:
         copy.wait_recv()
@@ -284,7 +281,10 @@
     smine[...] = units.astype(BF16)
     spread_start(smine, sgath, s_send, s_recv)
 
-    for j in range(early + 1, col_chunks):
+    for j in range(early):
+        moe_combine(j)
+        moe_b[j].start()
+    for j in range(early, col_chunks):
         moe_part(j)
     moe_c.start()
     for j in range(early, col_chunks):
@@ -452,17 +452,25 @@
     spread_done(smine, sgath, s_send, s_recv)
 
 
-def hand_on(moe_in, tgrad_in, ggrad_in, loss_in, moe, tgrad, ggrad, loss, sem):
-    copies = [
-        pltpu.make_async_copy(moe_in, moe, sem.at[0]),
-        pltpu.make_async_copy(tgrad_in, tgrad, sem.at[1]),
-    ]
-    for copy in copies:
-        copy.start()
+def hand_on(moe_in, tgrad_in, ggrad_in, loss_in, moe, tgrad, ggrad, loss, held, in_sem, out_sem):
+    chunks = in_sem.shape[1]
+    count = moe_in.shape[0] // chunks
+    loads, stores = [], []
+    for k in range(chunks):
+        at = pl.ds(k * count, count)
+        for which, (src, dst) in enumerate(((moe_in, moe), (tgrad_in, tgrad))):
+            slot = held.at[which, at]
+            loads.append(pltpu.make_async_copy(src.at[at], slot, in_sem.at[which, k]))
+            stores.append(pltpu.make_async_copy(slot, dst.at[at], out_sem.at[which, k]))
+    for load in loads:
+        load.start()
     ggrad[...] = ggrad_in[...]
     loss[...] = loss_in[...]
-    for copy in copies:
-        copy.wait()
+    for load, store in zip(loads, stores):
+        load.wait()
+        store.start()
+    for store in stores:
+        store.wait()
 
 
 def shards(
@@ -539,7 +547,7 @@
         out_shape=tuple(jax.ShapeDtypeStruct(a.shape, a.dtype) for a in (moe, tgrad, ggrad, loss)),
         in_specs=[hbm, hbm, vmem, vmem],
         out_specs=(hbm, hbm, vmem, vmem),
-        scratch_shapes=[dma((2,))],
+        scratch_shapes=[pltpu.VMEM((2, rows, width), BF16), dma((2, 4)), dma((2, 4))],
         compiler_params=pltpu.CompilerParams(vmem_limit_bytes=60 * 1024 * 1024),
     )(moe, tgrad, ggrad, loss)
     return moe, tgrad, ggrad.T, loss

time: 90 us -> 59.7 us (0.66)
  Pallas kernels: 88.5 us -> 58.2 us
    pallas_call x1, Pallas kernels: 34.7 us -> 3.93 us  [shards(): pl.pallas_call(hand_on, out_shape=tuple((jax.ShapeDtypeStruct(a.shape, a....]
where the time goes in v3:
time: 59.7 us; the launch traced here: 59.5 us
  Pallas kernels  58.2 us (97%)
  between operations  1.29 us (2%)
    pallas_call x1, Pallas kernels, shards(): pl.pallas_call(functools.partial(kernel, dims), out_shape=(jax.ShapeDtype...  54.2 us
    pallas_call x1, Pallas kernels, shards(): pl.pallas_call(hand_on, out_shape=tuple((jax.ShapeDtypeStruct(a.shape, a....  3.93 us

profile of v3, /device:TPU:0, one launch (start us, length us, event | category | flops | bytes accessed | tf_op | source)
XLA Modules:
  0.0 59.5 jit_solution(16653555657214775416)
XLA Ops:
  1.3 54.2 %shard_map.120 = (bf16[128,2048]{1,0:T(8,128)(2,1)}, bf16[128,2048]{1,0:T(8,128)(2,1)}, f32[2,128]{1,0:T(2,128)}, f32[1,1]{1,0:T(1,128)}) custom-call(bf16[128,2048]{1,0:T(8,128)(2,1)} %tok_ref.1, bf16[1,2048,768]{2,1,0:T(8,128)(2,1)} %wg_hbm.1, bf16[1,2048,768]{2,1,0:T(8,128)(2,1)} %wu_hbm.1, bf16[1,768,2048]{2,1,0:T(8,128)(2,1)} %wd_hbm.1, ...), custom_call_target="tpu_custom_call" | custom-call | tf_op jit(solution)/shard_map/pallas_call | solution.py:493
  55.5 3.9 %shard_map.121 = (bf16[128,2048]{1,0:T(8,128)(2,1)}, bf16[128,2048]{1,0:T(8,128)(2,1)}, f32[2,128]{1,0:T(2,128)}, f32[1,1]{1,0:T(1,128)}) custom-call(bf16[128,2048]{1,0:T(8,128)(2,1)} %get-tuple-element.12.moe_in, bf16[128,2048]{1,0:T(8,128)(2,1)} %get-tuple-element.13.tgrad_in, f32[2,128]{1,0:T(2,128)} %get-tuple-element.14.ggrad_in, ...), custom_call_target="tpu_custom_call" | custom-call | tf_op jit(solution)/shard_map/pallas_call | solution.py:545

commit v4 on v3

--- a/solution.py
+++ b/solution.py
@@ -44,7 +44,7 @@
     cbuf, crecv, slab, tmine, smine, tgath, sgath, tmat, smat, unit_buf,
     ogmine, ogbuf, ogmat, hgpad, ggsend, ggrecv,
     s_a, r_a, s_b, r_b, s_c, r_c, keep0, keep2,
-    out_v, send_sem, recv_sem, t_send, t_recv, s_send, s_recv, loc_sem, out_sem,
+    out_v, send_sem, recv_sem, t_send, t_recv, s_send, s_recv, loc_sem, tok_sem, out_sem,
 ):
     dp, ex, rows, width, ff, nq, npas, rp, tok_chunks, col_chunks = dims
     me = lax.axis_index("dp")
@@ -81,14 +81,17 @@
         started.append(copy)
         return copy
 
-    loads = [
-        pltpu.make_async_copy(tok_ref, xbuf.at[pl.ds(0, rows)], loc_sem.at[0]),
-        pltpu.make_async_copy(wg_hbm.at[0], wg, loc_sem.at[1]),
-        pltpu.make_async_copy(wu_hbm.at[0], wu, loc_sem.at[2]),
-        pltpu.make_async_copy(wd_hbm.at[0], wd, loc_sem.at[3]),
-    ]
-    for load in loads:
-        load.start()
+    tok_load = pltpu.make_async_copy(tok_ref, xbuf.at[pl.ds(0, rows)], tok_sem)
+    tok_load.start()
+    weight_parts = loc_sem.shape[1]
+    loads = []
+    for which, (src, dst) in enumerate(((wg_hbm, wg), (wu_hbm, wu), (wd_hbm, wd))):
+        count = dst.shape[0] // weight_parts
+        for k in range(weight_parts):
+            at = pl.ds(k * count, count)
+            load = pltpu.make_async_copy(src.at[0, at], dst.at[at], loc_sem.at[which, k])
+            load.start()
+            loads.append(load)
 
     barrier = pltpu.get_barrier_semaphore()
     for peer in peers[1:]:
@@ -188,9 +191,9 @@
 
         lax.fori_loop(0, ff // tile, body, 0)
 
-    loads[0].wait()
-    loads[1].wait()
-    loads[2].wait()
+    tok_load.wait()
+    for load in loads[: 2 * weight_parts]:
+        load.wait()
     sib_copy.wait_recv()
     forward(0, 2 * rows)
     forward_copies = []
@@ -219,7 +222,8 @@
             wf[s * rp : (s + 1) * rp, start : start + count] = weights[:, token : token + count]
     for s in range(ex):
         wt[s * rows : (s + 1) * rows, :] = jnp.transpose(wf[:, s * rows : (s + 1) * rows])
-    loads[3].wait()
+    for load in loads[2 * weight_parts :]:
+        load.wait()
 
     for copy in forward_copies[tok_chunks // 2 :]:
         copy.wait_recv()
@@ -264,7 +268,7 @@
         moe_a[j].wait_recv()
         s_b[0, j] = (keep2[j] + r_a[0, j].astype(F32)).astype(BF16)
 
-    early = col_chunks // 2
+    early = (3 * col_chunks) // 8
     for j in range(early):
         moe_part(j)
 
@@ -380,6 +384,7 @@
         s_b[1, j] = (keep2[j] + r_a[1, j].astype(F32)).astype(BF16)
         tg_b[j].start()
 
+    lag = 3
     gate_part, up_part = back_rows(2 * rows, 2 * rows)
     for j in range(col_chunks):
         at = pl.ds(j * dc, dc)
@@ -390,9 +395,10 @@
             shifted = part[start - 2 * rows : start - 2 * rows + count]
             s_a[1, j, token : token + count] = shifted.astype(BF16)
         tg_a[j].start()
-        if j:
-            combine(j - 1)
-    combine(col_chunks - 1)
+        if j >= lag:
+            combine(j - lag)
+    for j in range(col_chunks - lag, col_chunks):
+        combine(j)
 
     scores = mm_last(hg, hid[...])
     gg_copies = [remote(ggsend.at[s], ggrecv.at[s], peers[s]) for s in range(1, ex)]
@@ -452,7 +458,10 @@
     spread_done(smine, sgath, s_send, s_recv)
 
 
-def hand_on(moe_in, tgrad_in, ggrad_in, loss_in, moe, tgrad, ggrad, loss, held, in_sem, out_sem):
+def hand_on(
+    moe_in, tgrad_in, ggrad_in, loss_in, moe, tgrad, ggrad, loss,
+    held, held_ggrad, held_loss, in_sem, out_sem, small_sem,
+):
     chunks = in_sem.shape[1]
     count = moe_in.shape[0] // chunks
     loads, stores = [], []
@@ -462,10 +471,13 @@
             slot = held.at[which, at]
             loads.append(pltpu.make_async_copy(src.at[at], slot, in_sem.at[which, k]))
             stores.append(pltpu.make_async_copy(slot, dst.at[at], out_sem.at[which, k]))
+    for k, (src, slot, dst) in enumerate(
+        ((ggrad_in, held_ggrad, ggrad), (loss_in, held_loss, loss))
+    ):
+        loads.append(pltpu.make_async_copy(src, slot, small_sem.at[0, k]))
+        stores.append(pltpu.make_async_copy(slot, dst, small_sem.at[1, k]))
     for load in loads:
         load.start()
-    ggrad[...] = ggrad_in[...]
-    loss[...] = loss_in[...]
     for load, store in zip(loads, stores):
         load.wait()
         store.start()
@@ -482,7 +494,7 @@
     nq = teacher_queries.shape[1]
     npas = teacher_passages.shape[1]
     rp = -(-(nq + npas + 1) // 4) * 4
-    tok_chunks, col_chunks = 4, 4
+    tok_chunks, col_chunks = 4, 8
     dc = width // col_chunks
     dims = (dp, ex, rows, width, ff, nq, npas, rp, tok_chunks, col_chunks)
     copies = 2 * tok_chunks + 1 + 4 * (ex - 1) + 1 + 2 * col_chunks + 3 * col_chunks
@@ -533,7 +545,7 @@
             pltpu.VMEM((2, rows, width), BF16),
             dma((copies,)), dma((copies,)),
             dma((dp,)), dma((dp,)), dma((dp,)), dma((dp,)),
-            dma((4,)), dma((2, col_chunks)),
+            dma((3, 4)), dma, dma((2, col_chunks)),
         ],
         compiler_params=pltpu.CompilerParams(
             collective_id=0, has_side_effects=True, vmem_limit_bytes=60 * 1024 * 1024
@@ -545,9 +557,14 @@
     moe, tgrad, ggrad, loss = pl.pallas_call(
         hand_on,
         out_shape=tuple(jax.ShapeDtypeStruct(a.shape, a.dtype) for a in (moe, tgrad, ggrad, loss)),
-        in_specs=[hbm, hbm, vmem, vmem],
-        out_specs=(hbm, hbm, vmem, vmem),
-        scratch_shapes=[pltpu.VMEM((2, rows, width), BF16), dma((2, 4)), dma((2, 4))],
+        in_specs=[hbm] * 4,
+        out_specs=(hbm,) * 4,
+        scratch_shapes=[
+            pltpu.VMEM((2, rows, width), BF16),
+            pltpu.VMEM(ggrad.shape, F32),
+            pltpu.VMEM(loss.shape, F32),
+            dma((2, 2)), dma((2, 2)), dma((2, 2)),
+        ],
         compiler_params=pltpu.CompilerParams(vmem_limit_bytes=60 * 1024 * 1024),
     )(moe, tgrad, ggrad, loss)
     return moe, tgrad, ggrad.T, loss

time: 59.7 us -> 60.6 us (1.015)
  Pallas kernels: 58.2 us -> 59 us
    pallas_call x1, Pallas kernels: 54.2 us -> 56.4 us  [shards(): pl.pallas_call(functools.partial(kernel, dims), out_shape=(jax.ShapeDtype...]
    pallas_call x1, Pallas kernels: 3.93 us -> 2.65 us  [shards(): pl.pallas_call(hand_on, out_shape=tuple((jax.ShapeDtypeStruct(a.shape, a....]
where the time goes in v4:
time: 60.6 us; the launch traced here: 60.3 us
  Pallas kernels  59 us (97%)
  between operations  1.29 us (2%)
    pallas_call x1, Pallas kernels, shards(): pl.pallas_call(functools.partial(kernel, dims), out_shape=(jax.ShapeDtype...  56.4 us
    pallas_call x1, Pallas kernels, shards(): pl.pallas_call(hand_on, out_shape=tuple((jax.ShapeDtypeStruct(a.shape, a....  2.65 us

profile of v4, /device:TPU:0, one launch (start us, length us, event | category | flops | bytes accessed | tf_op | source)
XLA Modules:
  0.0 60.3 jit_solution(1441750005211080928)
XLA Ops:
  1.3 56.4 %shard_map.120 = (bf16[128,2048]{1,0:T(8,128)(2,1)}, bf16[128,2048]{1,0:T(8,128)(2,1)}, f32[2,128]{1,0:T(2,128)}, f32[1,1]{1,0:T(1,128)}) custom-call(bf16[128,2048]{1,0:T(8,128)(2,1)} %tok_ref.1, bf16[1,2048,768]{2,1,0:T(8,128)(2,1)} %wg_hbm.1, bf16[1,2048,768]{2,1,0:T(8,128)(2,1)} %wu_hbm.1, bf16[1,768,2048]{2,1,0:T(8,128)(2,1)} %wd_hbm.1, ...), custom_call_target="tpu_custom_call" | custom-call | tf_op jit(solution)/shard_map/pallas_call | solution.py:505
  57.7 2.6 %shard_map.121 = (bf16[128,2048]{1,0:T(8,128)(2,1)}, bf16[128,2048]{1,0:T(8,128)(2,1)}, f32[2,128]{1,0:T(2,128)}, f32[1,1]{1,0:T(1,128)}) custom-call(bf16[128,2048]{1,0:T(8,128)(2,1)} %get-tuple-element.12.moe_in, bf16[128,2048]{1,0:T(8,128)(2,1)} %get-tuple-element.13.tgrad_in, f32[2,128]{1,0:T(2,128)} %get-tuple-element.14.ggrad_in, ...), custom_call_target="tpu_custom_call" | custom-call | tf_op jit(solution)/shard_map/pallas_call | solution.py:557

commit v5 on v4

--- a/solution.py
+++ b/solution.py
@@ -81,6 +81,18 @@
         started.append(copy)
         return copy
 
+    barrier = pltpu.get_barrier_semaphore()
+    for peer in peers[1:]:
+        pl.semaphore_signal(barrier, inc=1, device_id=(me, peer), device_id_type=MESH)
+
+    def greet(off, carry):
+        pl.semaphore_signal(
+            barrier, inc=1, device_id=(lax.rem(me + off, dp), my_e), device_id_type=MESH
+        )
+        return carry
+
+    lax.fori_loop(1, dp, greet, 0)
+
     tok_load = pltpu.make_async_copy(tok_ref, xbuf.at[pl.ds(0, rows)], tok_sem)
     tok_load.start()
     weight_parts = loc_sem.shape[1]
@@ -92,18 +104,6 @@
             load = pltpu.make_async_copy(src.at[0, at], dst.at[at], loc_sem.at[which, k])
             load.start()
             loads.append(load)
-
-    barrier = pltpu.get_barrier_semaphore()
-    for peer in peers[1:]:
-        pl.semaphore_signal(barrier, inc=1, device_id=(me, peer), device_id_type=MESH)
-
-    def greet(off, carry):
-        pl.semaphore_signal(
-            barrier, inc=1, device_id=(lax.rem(me + off, dp), my_e), device_id_type=MESH
-        )
-        return carry
-
-    lax.fori_loop(1, dp, greet, 0)
 
     ids = ids_ref[...]
     probs = probs_ref[...].astype(F32)
@@ -197,102 +197,17 @@
     sib_copy.wait_recv()
     forward(0, 2 * rows)
     forward_copies = []
-    for k in range(tok_chunks):
-        token_copies[k].wait_recv()
-        copy = remote(
-            xbuf.at[pl.ds(far(2, k), chunk_rows)], xbuf.at[pl.ds(far(3, k), chunk_rows)], sib
-        )
-        copy.start()
-        forward_copies.append(copy)
-        if k == tok_chunks // 2 - 1:
-            for copy in forward_copies:
-                copy.wait_recv()
-            forward(2 * rows, rows)
-
-    for copy in meta_copies:
-        copy.wait_recv()
-    t_at = iota((rp, rows), 1)
-    segment = jnp.where(t_at < nq * QLEN, t_at // QLEN, nq + (t_at - nq * QLEN) // PLEN)
-    member = segment == iota((rp, rows), 0)
-    wf[...] = jnp.zeros_like(wf)
-    for s in range(ex):
-        prow = jnp.sum(jnp.where(iota((8, rows), 0) == my_e, meta[s], 0.0), axis=0, keepdims=True)
-        weights = jnp.where(member, prow, 0.0)
-        for start, count, token in places[s]:
-            wf[s * rp : (s + 1) * rp, start : start + count] = weights[:, token : token + count]
-    for s in range(ex):
-        wt[s * rows : (s + 1) * rows, :] = jnp.transpose(wf[:, s * rows : (s + 1) * rows])
-    for load in loads[2 * weight_parts :]:
-        load.wait()
-
-    for copy in forward_copies[tok_chunks // 2 :]:
-        copy.wait_recv()
-    forward(3 * rows, rows)
-
-    nseg = ex * rp
-    pooled_hid = mm(wf[0:nseg, :].astype(BF16), hid[...])
-    high = pooled_hid.astype(BF16)
-    low = (pooled_hid - high.astype(F32)).astype(BF16)
-    both = jnp.concatenate([high, low], axis=0)
-
-    def pooled_cols(j, carry):
-        cols = pl.ds(pl.multiple_of(j * dc, dc), dc)
-        part = mm(both, wd[:, cols])
-        part = part[0:nseg] + part[nseg:]
-        for s in range(ex):
-            cbuf[s, :, cols] = part[s * rp : (s + 1) * rp, :].astype(BF16)
-        return carry
-
-    lax.fori_loop(0, col_chunks, pooled_cols, 0)
-    pooled_copies = [remote(cbuf.at[s], crecv.at[s], peers[s]) for s in range(1, ex)]
-    for s in (2, 3, 1):
-        pooled_copies[s - 1].start()
-
-    pcol = jnp.sum(wt[...], axis=1, keepdims=True)
-
-    moe_a = [remote(s_a.at[0, j], r_a.at[0, j], sib) for j in range(col_chunks)]
-    moe_b = [remote(s_b.at[0, j], r_b.at[0, j], cross) for j in range(col_chunks)]
-    moe_c = remote(s_c.at[0], r_c.at[0], sib)
-
-    def moe_part(j):
-        part = mm(hid[...], wd[:, j * dc : (j + 1) * dc]) * pcol
-        keep0[0, j] = part[0:rows]
-        s_c[0, j] = part[rows : 2 * rows].astype(BF16)
-        for start, count, token in places[2]:
-            keep2[j, token : token + count] = part[start : start + count]
-        for start, count, token in places[3]:
-            s_a[0, j, token : token + count] = part[start : start + count].astype(BF16)
-        moe_a[j].start()
-
-    def moe_combine(j):
-        moe_a[j].wait_recv()
-        s_b[0, j] = (keep2[j] + r_a[0, j].astype(F32)).astype(BF16)
-
-    early = (3 * col_chunks) // 8
-    for j in range(early):
-        moe_part(j)
-
-    for copy in pooled_copies:
-        copy.wait_recv()
-    row_at = iota((rp, 1), 0)
-    is_query = row_at < nq
-    total = cbuf[0].astype(F32)
-    for s in range(1, ex):
-        total += crecv[s].astype(F32)
-    pooled = total * jnp.where(is_query, 1.0 / QLEN, 1.0 / PLEN)
-    units, inverse = unit_rows(pooled)
-    unit_buf[...] = units
-    smine[...] = units.astype(BF16)
-    spread_start(smine, sgath, s_send, s_recv)
-
-    for j in range(early):
-        moe_combine(j)
-        moe_b[j].start()
-    for j in range(early, col_chunks):
-        moe_part(j)
-    moe_c.start()
-    for j in range(early, col_chunks):
-        moe_combine(j)
+
+    def hand_over(first, last):
+        for k in range(first, last):
+            token_copies[k].wait_recv()
+            copy = remote(
+                xbuf.at[pl.ds(far(2, k), chunk_rows)], xbuf.at[pl.ds(far(3, k), chunk_rows)], sib
+            )
+            copy.start()
+            forward_copies.append(copy)
+
+    hand_over(0, tok_chunks // 2)
 
     spread_wait(tmine, tgath, t_send, t_recv)
     for i in range(dp):
@@ -322,6 +237,92 @@
     teacher_total = jnp.sum(teacher_exp, axis=1, keepdims=True)
     row_live = (iota((n, 1), 0) % rp) < nq
     teacher_total = jnp.where(row_live, teacher_total, 1.0)
+
+    for copy in forward_copies:
+        copy.wait_recv()
+    forward(2 * rows, rows)
+    hand_over(tok_chunks // 2, tok_chunks)
+
+    for copy in meta_copies:
+        copy.wait_recv()
+    t_at = iota((rp, rows), 1)
+    segment = jnp.where(t_at < nq * QLEN, t_at // QLEN, nq + (t_at - nq * QLEN) // PLEN)
+    member = segment == iota((rp, rows), 0)
+    wf[...] = jnp.zeros_like(wf)
+    for s in range(ex):
+        prow = jnp.sum(jnp.where(iota((8, rows), 0) == my_e, meta[s], 0.0), axis=0, keepdims=True)
+        weights = jnp.where(member, prow, 0.0)
+        for start, count, token in places[s]:
+            wf[s * rp : (s + 1) * rp, start : start + count] = weights[:, token : token + count]
+    for s in range(ex):
+        wt[s * rows : (s + 1) * rows, :] = jnp.transpose(wf[:, s * rows : (s + 1) * rows])
+    for load in loads[2 * weight_parts :]:
+        load.wait()
+
+    for copy in forward_copies[tok_chunks // 2 :]:
+        copy.wait_recv()
+    forward(3 * rows, rows)
+
+    nseg = ex * rp
+    pooled_hid = mm(wf[0:nseg, :].astype(BF16), hid[...])
+    high = pooled_hid.astype(BF16)
+    low = (pooled_hid - high.astype(F32)).astype(BF16)
+    both = jnp.concatenate([high, low], axis=0)
+
+    def pooled_cols(j, carry):
+        cols = pl.ds(pl.multiple_of(j * dc, dc), dc)
+        part = mm(both, wd[:, cols])
+        part = part[0:nseg] + part[nseg:]
+        for s in range(ex):
+            cbuf[s, :, cols] = part[s * rp : (s + 1) * rp, :].astype(BF16)
+        return carry
+
+    lax.fori_loop(0, col_chunks, pooled_cols, 0)
+    pooled_copies = [remote(cbuf.at[s], crecv.at[s], peers[s]) for s in range(1, ex)]
+    for s in (2, 3, 1):
+        pooled_copies[s - 1].start()
+
+    pcol = jnp.sum(wt[...], axis=1, keepdims=True)
+
+    moe_a = [remote(s_a.at[0, j], r_a.at[0, j], sib) for j in range(col_chunks)]
+    moe_b = [remote(s_b.at[0, j], r_b.at[0, j], cross) for j in range(col_chunks)]
+    moe_c = remote(s_c.at[0], r_c.at[0], sib)
+
+    def moe_part(j):
+        part = mm(hid[...], wd[:, j * dc : (j + 1) * dc]) * pcol
+        keep0[0, j] = part[0:rows]
+        s_c[0, j] = part[rows : 2 * rows].astype(BF16)
+        for start, count, token in places[2]:
+            keep2[j, token : token + count] = part[start : start + count]
+        for start, count, token in places[3]:
+            s_a[0, j, token : token + count] = part[start : start + count].astype(BF16)
+        moe_a[j].start()
+
+    def moe_combine(j):
+        moe_a[j].wait_recv()
+        s_b[0, j] = (keep2[j] + r_a[0, j].astype(F32)).astype(BF16)
+
+    early = col_chunks // 2
+    for j in range(early):
+        moe_part(j)
+
+    for copy in pooled_copies:
+        copy.wait_recv()
+    row_at = iota((rp, 1), 0)
+    is_query = row_at < nq
+    total = cbuf[0].astype(F32)
+    for s in range(1, ex):
+        total += crecv[s].astype(F32)
+    pooled = total * jnp.where(is_query, 1.0 / QLEN, 1.0 / PLEN)
+    units, inverse = unit_rows(pooled)
+    unit_buf[...] = units
+    smine[...] = units.astype(BF16)
+    spread_start(smine, sgath, s_send, s_recv)
+
+    for j in range(early):
+        moe_combine(j)
+        moe_b[j].start()
+    moe_part(early)
 
     spread_wait(smine, sgath, s_send, s_recv)
     for i in range(dp):
@@ -354,8 +355,12 @@
     og_copies = [remote(ogmine, ogbuf.at[s], peers[s]) for s in range(1, ex)]
     for s in (2, 3, 1):
         og_copies[s - 1].start()
-    for copy in moe_b[early:]:
-        copy.start()
+    for j in range(early + 1, col_chunks):
+        moe_part(j)
+    moe_c.start()
+    for j in range(early, col_chunks):
+        moe_combine(j)
+        moe_b[j].start()
 
     hgpad[...] = jnp.zeros_like(hgpad)
     ogmat[0:rp, :] = grad
@@ -384,7 +389,7 @@
         s_b[1, j] = (keep2[j] + r_a[1, j].astype(F32)).astype(BF16)
         tg_b[j].start()
 
-    lag = 3
+    lag = 1
     gate_part, up_part = back_rows(2 * rows, 2 * rows)
     for j in range(col_chunks):
         at = pl.ds(j * dc, dc)
@@ -494,7 +499,7 @@
     nq = teacher_queries.shape[1]
     npas = teacher_passages.shape[1]
     rp = -(-(nq + npas + 1) // 4) * 4
-    tok_chunks, col_chunks = 4, 8
+    tok_chunks, col_chunks = 4, 4
     dc = width // col_chunks
     dims = (dp, ex, rows, width, ff, nq, npas, rp, tok_chunks, col_chunks)
     copies = 2 * tok_chunks + 1 + 4 * (ex - 1) + 1 + 2 * col_chunks + 3 * col_chunks
@@ -545,7 +550,7 @@
             pltpu.VMEM((2, rows, width), BF16),
             dma((copies,)), dma((copies,)),
             dma((dp,)), dma((dp,)), dma((dp,)), dma((dp,)),
-            dma((3, 4)), dma, dma((2, col_chunks)),
+            dma((3, 1)), dma, dma((2, col_chunks)),
         ],
         compiler_params=pltpu.CompilerParams(
             collective_id=0, has_side_effects=True, vmem_limit_bytes=60 * 1024 * 1024

time: 60.6 us -> 58.4 us (0.964)
  Pallas kernels: 59 us -> 56.9 us
    pallas_call x1, Pallas kernels: 56.4 us -> 54.2 us  [shards(): pl.pallas_call(functools.partial(kernel, dims), out_shape=(jax.ShapeDtype...]
where the time goes in v5:
time: 58.4 us; the launch traced here: 58.2 us
  Pallas kernels  56.9 us (97%)
  between operations  1.29 us (2%)
    pallas_call x1, Pallas kernels, shards(): pl.pallas_call(functools.partial(kernel, dims), out_shape=(jax.ShapeDtype...  54.2 us
    pallas_call x1, Pallas kernels, shards(): pl.pallas_call(hand_on, out_shape=tuple((jax.ShapeDtypeStruct(a.shape, a....  2.65 us

profile of v5, /device:TPU:0, one launch (start us, length us, event | category | flops | bytes accessed | tf_op | source)
XLA Modules:
  0.0 58.2 jit_solution(4793915111388195502)
XLA Ops:
  1.3 54.2 %shard_map.120 = (bf16[128,2048]{1,0:T(8,128)(2,1)}, bf16[128,2048]{1,0:T(8,128)(2,1)}, f32[2,128]{1,0:T(2,128)}, f32[1,1]{1,0:T(1,128)}) custom-call(bf16[128,2048]{1,0:T(8,128)(2,1)} %tok_ref.1, bf16[1,2048,768]{2,1,0:T(8,128)(2,1)} %wg_hbm.1, bf16[1,2048,768]{2,1,0:T(8,128)(2,1)} %wu_hbm.1, bf16[1,768,2048]{2,1,0:T(8,128)(2,1)} %wd_hbm.1, ...), custom_call_target="tpu_custom_call" | custom-call | tf_op jit(solution)/shard_map/pallas_call | solution.py:510
  55.5 2.6 %shard_map.121 = (bf16[128,2048]{1,0:T(8,128)(2,1)}, bf16[128,2048]{1,0:T(8,128)(2,1)}, f32[2,128]{1,0:T(2,128)}, f32[1,1]{1,0:T(1,128)}) custom-call(bf16[128,2048]{1,0:T(8,128)(2,1)} %get-tuple-element.12.moe_in, bf16[128,2048]{1,0:T(8,128)(2,1)} %get-tuple-element.13.tgrad_in, f32[2,128]{1,0:T(2,128)} %get-tuple-element.14.ggrad_in, ...), custom_call_target="tpu_custom_call" | custom-call | tf_op jit(solution)/shard_map/pallas_call | solution.py:562
